TPU v7x, 128 devices: a whole 4x4x4 slice. The times are simulated.
128 devices in a mesh: dp: 32 (over z, x, core), tp: 4 (over y).
Axes of the slice: x: 4, y: 4, z: 4, core: 2. Of those that a mesh axis runs over, the one named last changes fastest.
Arguments:
- queries: bfloat16 [512, 128, 576], P(('dp', 'tp')), may hold values from -16 to 16
- latent_cache: bfloat16 [512, 1024, 576], P(('dp', 'tp')), may hold values from -4 to 4
- lengths: int32 [512], P(('dp', 'tp')), may hold values from 2 to 1024, as said below
- uv_weight: bfloat16 [128, 512, 128], P('tp'), may hold values from -0.25 to 0.25
- out_weight: bfloat16 [16384, 7168], P('tp', 'dp'), may hold values from -0.375 to 0.375
- residual: bfloat16 [512, 7168], P(None, 'dp'), may hold values from -6 to 6
- norm_gain: float32 [7168], replicated, may hold values from 0.1 to 1.9
- gate_weight: bfloat16 [32, 7168, 1024], P('dp', None, 'tp'), may hold values from -0.0625 to 0.0625
- up_weight: bfloat16 [32, 7168, 1024], P('dp', None, 'tp'), may hold values from -0.0625 to 0.0625
- down_weight: bfloat16 [32, 1024, 7168], P('dp', 'tp'), may hold values from -0.1875 to 0.1875
- routes: int32 [512, 8], replicated, may hold values from 0 to 31, all different within a row; in each aligned block of 512 rows (0 to 511, 512 to 1023, ...) at most 384 rows name the same one
- route_weights: float32 [512, 8], replicated, may hold values from 0.1 to 0.6
Outputs:
- block_output: bfloat16 [512, 7168], P('tp', 'dp')
Inputs may be any that keep to these rules, and one draw needn't show every extreme that they name: `routes`: each row names 8 different experts; no expert is named by more than 384 of the 512 rows, a bound that some block reaches. `lengths`: some row uses all 1024 positions.
All inputs are finite; a program needn't handle non-finite values.
Results may differ from a plain program's by a relative error of at most 0.01.
Values may be sent and summed in bfloat16 or wider, within the bound.
A program may use at most 128 MiB of HBM per device.

v0:
```python
import jax
import jax.numpy as jnp
from jax import lax
from jax.sharding import PartitionSpec as P

LAT = 512


score_scale = 192.0 ** (-0.5)
epsilon = 1e-06


def attend_rows(queries, latent_cache, lengths):
    scores = (
        jnp.einsum("rhc,rtc->rht", queries, latent_cache, preferred_element_type=jnp.float32)
        * score_scale
    )
    usable = (jnp.arange(latent_cache.shape[1], dtype=jnp.int32)[None, :] < lengths[:, None])[
        :, None, :
    ]
    peak_score = jnp.max(jnp.where(usable, scores, -1e30), axis=2, keepdims=True)
    exp_scores = jnp.where(usable, jnp.exp(scores - peak_score), 0.0)
    row_total = jnp.sum(exp_scores, axis=2, keepdims=True)
    summed = jnp.einsum(
        "rht,rtc->rhc",
        exp_scores.astype(jnp.bfloat16),
        latent_cache[:, :, :LAT],
        preferred_element_type=jnp.float32,
    )
    return (summed / row_total).astype(jnp.bfloat16)


def route_tables(routes, route_weights, experts):
    expert_ids = jnp.arange(experts, dtype=jnp.int32)
    matches = (routes[:, :, None] == expert_ids[None, None, :]).astype(jnp.float32)
    hit_table = jnp.sum(matches, axis=1)
    weight_table = jnp.sum(route_weights[:, :, None] * matches, axis=1)
    total_rows = routes.shape[0]
    row_ids = jnp.arange(total_rows, dtype=jnp.int32)
    earlier = (row_ids[None, :] < row_ids[:, None]).astype(jnp.float32)
    before = jnp.dot(earlier, hit_table, precision=lax.Precision.HIGHEST)
    return (hit_table, weight_table, before)


def slot_select(hit_table, before, count):
    slot_ids = jnp.arange(count, dtype=jnp.int32).astype(jnp.float32)
    taken = (hit_table.T > 0.5)[:, None, :]
    return jnp.logical_and(taken, before.T[:, None, :] == slot_ids[None, :, None])


def rms_scaled(rows, norm_gain):
    values = rows.astype(jnp.float32)
    inverse_rms = lax.rsqrt(jnp.mean(values * values, axis=1, keepdims=True) + epsilon)
    return (values * inverse_rms * norm_gain).astype(jnp.bfloat16)


def local(
    queries,
    latent_cache,
    lengths,
    uv_weight,
    out_weight,
    residual,
    norm_gain,
    gate_weight,
    up_weight,
    down_weight,
    routes,
    route_weights,
):
    dp_count = lax.axis_size("dp")
    tp_count = lax.axis_size("tp")
    context = attend_rows(queries, latent_cache, lengths)
    by_head = lax.all_to_all(context, "tp", split_axis=1, concat_axis=0, tiled=True)
    head_out = jnp.einsum(
        "rhc,hcv->rhv", by_head, uv_weight, preferred_element_type=jnp.float32
    ).astype(jnp.bfloat16)
    head_out = head_out.reshape(head_out.shape[0], head_out.shape[1] * head_out.shape[2])
    attn_part = jnp.dot(
        lax.all_gather(head_out, "dp", axis=0, tiled=True),
        out_weight,
        preferred_element_type=jnp.float32,
    )
    attn_full = lax.psum(attn_part, "tp")
    hidden = (residual.astype(jnp.float32) + attn_full).astype(jnp.bfloat16)
    total_rows = routes.shape[0]
    capacity = min(total_rows, 3 * total_rows * routes.shape[1] // dp_count)
    hit_table, weight_table, before = route_tables(routes, route_weights, dp_count)
    local_width = hidden.shape[1]
    full_select = slot_select(hit_table, before, capacity)
    outgoing = jnp.einsum(
        "esr,rd->esd", full_select.astype(jnp.bfloat16), hidden, preferred_element_type=jnp.float32
    ).astype(jnp.bfloat16)
    outgoing = outgoing.reshape(dp_count * capacity, local_width)
    arrived = lax.all_to_all(outgoing, "dp", split_axis=0, concat_axis=1, tiled=True)
    normed = rms_scaled(arrived, norm_gain)
    gate_proj = jnp.dot(normed, gate_weight[0], preferred_element_type=jnp.float32)
    up_proj = jnp.dot(normed, up_weight[0], preferred_element_type=jnp.float32)
    activated = (jax.nn.silu(gate_proj) * up_proj).astype(jnp.bfloat16)
    partial_value = jnp.dot(activated, down_weight[0], preferred_element_type=jnp.float32).astype(
        jnp.bfloat16
    )
    returned = lax.all_to_all(partial_value, "dp", split_axis=1, concat_axis=0, tiled=True)
    back_select = slot_select(hit_table, before, capacity)
    combiner = back_select.astype(jnp.float32) * weight_table.T[:, None, :]
    moe_part = jnp.einsum(
        "esr,esd->rd",
        combiner,
        returned.astype(jnp.float32).reshape(dp_count, capacity, local_width),
        precision=lax.Precision.HIGHEST,
    )
    moe_rows = lax.psum_scatter(moe_part, "tp", scatter_dimension=0, tiled=True)
    block_rows = total_rows // tp_count
    own_hidden = lax.dynamic_slice_in_dim(hidden, lax.axis_index("tp") * block_rows, block_rows, 0)
    return (own_hidden.astype(jnp.float32) + moe_rows).astype(jnp.bfloat16)


def solution(mesh):
    placed = (
        P(("dp", "tp"), None, None),
        P(("dp", "tp"), None, None),
        P(("dp", "tp")),
        P("tp", None, None),
        P("tp", "dp"),
        P(None, "dp"),
        P(),
        P("dp", None, "tp"),
        P("dp", None, "tp"),
        P("dp", "tp", None),
        P(),
        P(),
    )
    return jax.shard_map(
        local, mesh=mesh, in_specs=placed, out_specs=P("tp", "dp"), check_vma=False
    )
```

profile of v0, /device:TPU:0, one launch (start us, length us, event | category | flops | bytes accessed | tf_op | source)
XLA Modules:
  0.0 352.4 jit_solution(14123658033151265246)
XLA Ops:
  6.5 0.9 iota_compare_fusion.3
  7.4 6.6 %fusion.53 = (f32[4,128]{1,0:T(4,128)S(1)}, bf16[4,128,1024]{2,1,0:T(8,128)(2,1)S(1)}) fusion(pred[4,1024]{1,0:T(4,128)(4,1)S(1)} %iota_compare_fusion.3, bf16[4,128,576]{1,2,0:T(8,128)(2,1)} %param.12, bf16[4,1024,576]{1,2,0:T(8,128)(2,1)} %param.13), kind=kOutput, calls=%fused_computation.59 | convolution fusion | flops 1211630592 | bytes 6363136 | tf_op jit(solution)/shard_map/sub | solution.py:22
  14.0 3.8 %divide_convert_fusion = bf16[4,128,512]{2,1,0:T(8,128)(2,1)S(1)} fusion(bf16[4,1024,576]{1,2,0:T(8,128)(2,1)} %param.13, bf16[4,128,1024]{2,1,0:T(8,128)(2,1)S(1)} %get-tuple-element.8, f32[4,128]{1,0:T(4,128)S(1)} %get-tuple-element.7), kind=kOutput, calls=%fused_computation.38 | convolution fusion | flops 537395200 | bytes 5769216 | tf_op jit(solution)/shard_map/rht,rtc->rhc/dot_general | solution.py:24
  17.8 0.4 copy.32
  18.3 13.8 %all_to_all.44 = bf16[4,128,512]{2,0,1:T(4,128)(2,1)S(1)} all-to-all(bf16[4,128,512]{2,0,1:T(4,128)(2,1)S(1)} %copy.32), channel_id=1, replica_groups=mesh['dp'=32,'tp'=4] {'tp'}, dimensions={1} | all-to-all | bytes 1048576 | tf_op jit(solution)/shard_map/all_to_all | solution.py:74
  32.1 0.3 copy.40
  32.4 0.1 all_to_all.36
  32.5 2.8 fusion.39
  35.4 0.7 copy.41
  36.1 0.1 select_reduce_fusion.1
  36.2 46.7 %all-gather.2.cloned.1.call-done = bf16[512,4096]{1,0:T(8,128)(2,1)} async-done(((bf16[16,4096]{1,0:T(8,128)(2,1)}), bf16[512,4096]{1,0:T(8,128)(2,1)}) %all-gather.2.cloned.1.call-update) | async-done | bytes 4194320 | tf_op jit(solution)/shard_map/all_gather | solution.py:80
  82.9 4.4 %fusion.56 = f32[512,224]{0,1:T(8,128)} fusion(bf16[512,4096]{1,0:T(8,128)(2,1)} %all-gather.2.cloned.1.call-done, bf16[4096,224]{0,1:T(8,128)(2,1)S(1)} %copy-done), kind=kOutput, calls=%fused_computation.61 | convolution fusion | flops 939524096 | bytes 6488064 | tf_op jit(solution)/shard_map/dot_general | solution.py:79
  87.4 0.5 fusion.44
  87.9 41.5 %all-reduce.2.cloned.1.call-done = f32[512,224]{0,1:T(8,128)} async-done(((f32[512,224]{0,1:T(8,128)}), f32[512,224]{0,1:T(8,128)}) %all-reduce.2.cloned.1.call-update) | async-done | bytes 458768 | tf_op jit(solution)/shard_map/psum | solution.py:84
  129.4 1.1 add_convert_fusion
  130.5 8.1 %fusion.23 = bf16[32,384,224]{1,2,0:T(8,128)(2,1)} fusion(f32[32,512]{1,0:T(8,128)S(1)} %fusion.44, f32[384]{0:T(512)S(1)} %iota_convert_fusion, pred[32,512]{1,0:T(8,128)(4,1)S(1)} %compare_bitcast_fusion, bf16[512,224]{0,1:T(8,128)(2,1)S(1)} %add_convert_fusion), kind=kOutput, calls=%fused_computation.27 | convolution fusion | flops 2833907712 | bytes 5817856 | tf_op jit(solution)/shard_map/esr,rd->esd/dot_general | solution.py:91
  138.6 7.5 %all-to-all-start.1 = ((bf16[32,384,224]{1,2,0:T(8,128)(2,1)}), bf16[32,384,224]{1,2,0:T(8,128)(2,1)}, u32[]{:S(2)}, u32[]{:S(2)}) async-start(bf16[32,384,224]{1,2,0:T(8,128)(2,1)} %fusion.23), calls=%async_computation.1 | async-start | bytes 11010048 | tf_op jit(solution)/shard_map/all_to_all | solution.py:95
  146.1 0.2 reduce-scatter.2.cloned.1.call-start
  146.3 0.1 mul.71
  146.4 68.4 %all-to-all-done.1 = bf16[32,384,224]{1,2,0:T(8,128)(2,1)} async-done(((bf16[32,384,224]{1,2,0:T(8,128)(2,1)}), bf16[32,384,224]{1,2,0:T(8,128)(2,1)}, u32[]{:S(2)}, u32[]{:S(2)}) %all-to-all-start.1) | async-done | bytes 5505056 | tf_op jit(solution)/shard_map/all_to_all | solution.py:95
  214.8 3.8 %fusion.12 = f32[384]{0:T(512)S(1)} fusion(bf16[32,384,224]{1,2,0:T(8,128)(2,1)} %all-to-all-done.1), kind=kLoop, calls=%fused_computation.15 | loop fusion | flops 8257152 | bytes 5506560 | tf_op jit(solution)/shard_map/reduce_sum | solution.py:53
  218.6 4.3 %fusion.14 = bf16[32,384,224]{1,2,0:T(8,128)(2,1)S(1)} fusion(bf16[32,384,224]{1,2,0:T(8,128)(2,1)} %all-to-all-done.1, f32[32,224]{1,0:T(8,128)S(1)} %mul.71, f32[384]{0:T(512)S(1)} %add_rsqrt_fusion), kind=kLoop, calls=%fused_computation.17 | loop fusion | flops 11010048 | bytes 11040256 | tf_op jit(solution)/shard_map/convert_element_type | solution.py:54
  222.9 1.6 fusion.21
  224.6 0.4 copy-done.2
  225.0 1.6 fusion.36
  226.6 0.4 copy-done.3
  227.0 4.0 %convolution_convert_fusion = bf16[384,7168]{1,0:T(8,128)(2,1)} fusion(bf16[384,256]{1,0:T(8,128)(2,1)S(1)} %fusion.36, bf16[1,256,7168]{2,1,0:T(8,128)(2,1)S(1)} %copy-done.3), kind=kOutput, calls=%fused_computation.18 | convolution fusion | flops 1412038656 | bytes 9371648 | tf_op jit(solution)/shard_map/dot_general | solution.py:100
  231.0 8.3 %copy.35 = bf16[384,7168]{0,1:T(8,128)(2,1)} copy(bf16[384,7168]{1,0:T(8,128)(2,1)} %convolution_convert_fusion) | data formatting | bytes 11010048 | tf_op jit(solution)/shard_map/convert_element_type | solution.py:100
  239.3 69.2 %all_to_all.45 = bf16[384,32,224]{0,2,1:T(8,128)(2,1)S(1)} all-to-all(bf16[384,32,224]{0,2,1:T(8,128)(2,1)} %bitcast.57), channel_id=1, replica_groups=mesh['dp'=32,'tp'=4] {'dp'}, dimensions={1} | all-to-all | bytes 11010048 | tf_op jit(solution)/shard_map/all_to_all | solution.py:103
  308.4 16.8 %fusion.28 = f32[512,224]{0,1:T(8,128)} fusion(bf16[384,32,224]{0,2,1:T(8,128)(2,1)S(1)} %all_to_all.45, f32[32,512]{1,0:T(8,128)S(1)} %bitcast.61, f32[32,512]{1,0:T(8,128)S(1)} %fusion.44, f32[384]{0:T(512)S(1)} %iota_convert_fusion, pred[32,512]{1,0:T(8,128)(4,1)S(1)} %compare_bitcast_fusion), kind=kOutput, calls=%fused_computation.32 | convolution fusion | flops 16930308096 | bytes 6112768 | tf_op jit(solution)/shard_map/esr,esd->rd/dot_general | solution.py:106
  325.3 19.0 %reduce-scatter.2.cloned.1.call-done = f32[128,224]{0,1:T(8,128)} async-done(((f32[512,224]{0,1:T(8,128)}), f32[128,224]{0,1:T(8,128)}) %reduce-scatter.2.cloned.1.call-update) | async-done | bytes 114704 | tf_op jit(solution)/shard_map/reduce_scatter | solution.py:112
  344.3 1.5 add_convert_fusion.1
  (22 shorter events, 0.2 us)
Async XLA Ops:
  6.5 76.4 %copy-start = (bf16[4096,224]{0,1:T(8,128)(2,1)S(1)}, bf16[4096,224]{0,1:T(8,128)(2,1)}, u32[]{:S(2)}) copy-start(bf16[4096,224]{0,1:T(8,128)(2,1)} %param.16) | copy-start | bytes 5505028
  6.5 76.4 %all-gather.2.cloned.1.call-start = ((), (), s32[]{:S(2)}) async-start(), calls=%async_computation.4 | async-start | bytes 4325376 | tf_op jit(solution)/shard_map/all_gather | solution.py:80
  17.8 18.3 %copy-start.6 = (f32[512,8]{0,1:T(8,128)S(1)}, f32[512,8]{0,1:T(8,128)}, u32[]{:S(2)}) copy-start(f32[512,8]{0,1:T(8,128)} %param.23) | copy-start | bytes 49156
  17.8 18.3 %copy-start.7 = (s32[512,8]{0,1:T(8,128)S(1)}, s32[512,8]{0,1:T(8,128)}, u32[]{:S(2)}) copy-start(s32[512,8]{0,1:T(8,128)} %param.22) | copy-start | bytes 49156
  35.3 94.1 %copy-start.4 = (bf16[512,224]{0,1:T(8,128)(2,1)S(1)}, bf16[512,224]{0,1:T(8,128)(2,1)}, u32[]{:S(2)}) copy-start(bf16[512,224]{0,1:T(8,128)(2,1)} %param.17) | copy-start | bytes 688132
  36.1 93.4 %all-reduce.2.cloned.1.call-start = ((), (), s32[]{:S(2)}) async-start(), calls=%async_computation.5 | async-start | bytes 917504 | tf_op jit(solution)/shard_map/psum | solution.py:84
  138.6 7.7 %copy-start.5 = (f32[7168]{0:T(1024)S(1)}, f32[7168]{0:T(1024)}, u32[]{:S(2)}) copy-start(f32[7168]{0:T(1024)} %param.18) | copy-start | bytes 86020
  138.6 76.2 %all-to-all-start.1 = ((bf16[32,384,224]{1,2,0:T(8,128)(2,1)}), bf16[32,384,224]{1,2,0:T(8,128)(2,1)}, u32[]{:S(2)}, u32[]{:S(2)}) async-start(bf16[32,384,224]{1,2,0:T(8,128)(2,1)} %fusion.23), calls=%async_computation.1 | async-start | bytes 11010048 | tf_op jit(solution)/shard_map/all_to_all | solution.py:95
  146.1 198.2 %reduce-scatter.2.cloned.1.call-start = ((), (), s32[]{:S(2)}) async-start(), calls=%async_computation.6 | async-start | bytes 573440 | tf_op jit(solution)/shard_map/reduce_scatter | solution.py:112
  218.6 4.3 %copy-start.1 = (bf16[1,7168,256]{2,1,0:T(8,128)(2,1)S(1)}, bf16[1,7168,256]{2,1,0:T(8,128)(2,1)}, u32[]{:S(2)}) copy-start(bf16[1,7168,256]{2,1,0:T(8,128)(2,1)} %param.19) | copy-start | bytes 11010052
  222.9 2.0 copy-start.2
  225.0 2.0 copy-start.3
Sparse Core Ops, SparseCore 0:
  36.2 46.7 all-gather.1
  87.5 41.8 all-reduce.1
  325.4 18.8 reduce-scatter.1
where the time goes:
time: 353 us; the launch traced here: 352 us
  waiting for transfers between devices  176 us (50%)
  blocking collectives  83 us (24%)
  matrix products  50.3 us (14%)
  between operations  13.3 us (4%)
  other arithmetic  11.7 us (3%)
  local copies, waits for them, and re-layouts  10.7 us (3%)
  starting transfers between devices  7.74 us (2%)
    all_to_all x1, blocking collectives, local(): lax.all_to_all(partial_value, 'dp', split_axis=1, concat_axis=0, tiled=True)  69.2 us
    all_to_all x1, waiting for transfers between devices, local(): lax.all_to_all(outgoing, 'dp', split_axis=0, concat_axis=1, tiled=True)  68.4 us
    all_gather x1, waiting for transfers between devices, local(): lax.all_gather(head_out, 'dp', axis=0, tiled=True)  46.7 us
    psum x1, waiting for transfers between devices, local(): attn_full = lax.psum(attn_part, 'tp')  41.5 us
    reduce_scatter x1, waiting for transfers between devices, local(): moe_rows = lax.psum_scatter(moe_part, 'tp', scatter_dimension=0, tiled=True)  19 us
    dot_general x1, matrix products, local(): jnp.einsum('esr,esd->rd', combiner, returned.astype(jnp.float32).reshape(...  16.8 us
    all_to_all x1, blocking collectives, local(): lax.all_to_all(context, 'tp', split_axis=1, concat_axis=0, tiled=True)  13.8 us
    convert_element_type x1, local copies, waits for them, and re-layouts, local(): jnp.dot(activated, down_weight[0], preferred_element_type=jnp.float32)  8.27 us
  transfers between devices with their start and end apart: 4, of which 4 were waited for; matrix products, arithmetic and copies ran while one was open for 0% of the time, Pallas kernels for 0%

commit v1 on v0

v1 whole, which is shorter than its diff:
```python
import functools

import jax
import jax.numpy as jnp
from jax import lax
from jax.experimental import pallas as pl
from jax.experimental.pallas import tpu as pltpu
from jax.sharding import PartitionSpec as P

F32 = jnp.float32
BF16 = jnp.bfloat16
MESH = pl.DeviceIdType.MESH

LAT = 512
KEY = 576
CTX = 1024
HEADS = 128
OWN_HEADS = 32
VHEAD = 128
ROWS = 512
OWN_ROWS = 4
DP_ROWS = 16
TP_ROWS = 128
D = 7168
COLS = 224
HALF = 112
INNER = 4096
UNITS = 256
DP = 32

score_scale = 192.0 ** (-0.5)
epsilon = 1e-06

RIGHT = (0, 2)
LEFT = (1, 3)
ORDER = (0, 1, 3, 2)


def tn_dot(a, b):
    return lax.dot_general(a, b, (((0,), (0,)), ((), ())), preferred_element_type=F32)


def nt_dot(a, b):
    return lax.dot_general(a, b, (((1,), (1,)), ((), ())), preferred_element_type=F32)


class Place:
    def __init__(self):
        dp = lax.axis_index("dp")
        self.y = lax.axis_index("tp")
        self.d = dp
        self.c = lax.rem(dp, 2)
        self.x = lax.rem(dp // 2, 4)
        self.z = dp // 8

    def device(self, z=None, x=None, c=None, y=None):
        z = self.z if z is None else z
        x = self.x if x is None else x
        c = self.c if c is None else c
        y = self.y if y is None else y
        return ((z * 4 + x) * 2 + c, y)

    def sibling(self):
        return self.device(c=1 - self.c)

    def tp_peer(self, step):
        return self.device(y=lax.rem(self.y + step, 4))

    def first(self, half):
        return self.x if half == 0 else self.z

    def second(self, half):
        return self.z if half == 0 else self.x

    def first_peer(self, half, step):
        if half == 0:
            return self.device(x=lax.rem(self.x + step, 4))
        return self.device(z=lax.rem(self.z + step, 4))

    def second_peer(self, half, step):
        return self.first_peer(1 - half, step)

    def block(self, half, j, k, c):
        a = lax.rem(self.first(half) + j, 4)
        b = lax.rem(self.second(half) + k, 4)
        z, x = (b, a) if half == 0 else (a, b)
        return (z * 4 + x) * 2 + c


def remote(src, dst, send, recv, device):
    return pltpu.make_async_remote_copy(
        src_ref=src, dst_ref=dst, send_sem=send, recv_sem=recv, device_id=device, device_id_type=MESH
    )


def gather_plane(me, blk, send_sem, recv_sem, sib_send, sib_recv):
    sends = []
    count = [0, 0]

    def send(half, j, k, device, rj, rk):
        ref = blk(me.block(half, j, k, me.c), half)
        copy = remote(
            ref, ref, send_sem.at[half, count[half]], recv_sem.at[half, rj * 4 + rk], device
        )
        count[half] += 1
        copy.start()
        sends.append(copy)

    def to_sibling(half, j, k):
        ref = blk(me.block(half, j, k, me.c), half)
        copy = remote(
            ref, ref, sib_send.at[half, j * 4 + k], sib_recv.at[half, j * 4 + k], me.sibling()
        )
        copy.start()
        sends.append(copy)

    def arrived(half, j, k):
        ref = blk(me.block(half, j, k, me.c), half)
        remote(
            ref, ref, send_sem.at[half, 0], recv_sem.at[half, j * 4 + k], me.sibling()
        ).wait_recv()

    def second_axis(half, j):
        send(half, j, 0, me.second_peer(half, 1), j, 3)
        send(half, j, 0, me.second_peer(half, 3), j, 1)

    for half in range(2):
        for step in (1, 3, 2):
            send(half, 0, 0, me.first_peer(half, step), (4 - step) % 4, 0)
    for half in range(2):
        second_axis(half, 0)
        to_sibling(half, 0, 0)
    for j in (1, 3, 2):
        for half in range(2):
            arrived(half, j, 0)
            second_axis(half, j)
            to_sibling(half, j, 0)
    for j in ORDER:
        for half in range(2):
            arrived(half, j, 3)
            if j in RIGHT:
                send(half, j, 3, me.second_peer(half, 1), j, 2)
            to_sibling(half, j, 3)
            arrived(half, j, 1)
            if j in LEFT:
                send(half, j, 1, me.second_peer(half, 3), j, 2)
            to_sibling(half, j, 1)
    for j in ORDER:
        for half in range(2):
            arrived(half, j, 2)
            to_sibling(half, j, 2)
    for half in range(2):
        for j in range(4):
            for k in range(4):
                ref = blk(me.block(half, j, k, 1 - me.c), half)
                remote(
                    ref, ref, sib_send.at[half, 0], sib_recv.at[half, j * 4 + k], me.sibling()
                ).wait_recv()
    return sends


def kernel(
    lengths, q_hbm, cache_hbm, uv_hbm, out_w_hbm, residual_hbm, gain, gate_hbm, up_hbm, down_hbm,
    routes, route_weights, out,
    qv, cv, uv, out_w, res, gate_w, up_w, down_w,
    ctx, by_head, by_head_f, heads_all, part, part_b, part_r, hid, hid_t, gate_acc, up_acc,
    act, contrib, from_sib, pass_r, ring_r, line_r, plane_sum, plane_sum_b, tp_r, weight_row,
    load_sem, a2a_send, a2a_recv, ag_send, ag_recv, ag_sib_send, ag_sib_recv,
    rs_send, rs_recv, hy_send, hy_recv, ah_send, ah_recv, ah_sib_send, ah_sib_recv,
    sib_send, sib_recv, pass_send, pass_recv, ring_send, ring_recv, line_send, line_recv,
    tp_send, tp_recv,
):
    me = Place()
    y, d = me.y, me.d
    own_lanes = pl.ds(pl.multiple_of(y * TP_ROWS, TP_ROWS), TP_ROWS)

    loads = {}

    def load(name, src, dst, index):
        copy = pltpu.make_async_copy(src, dst, load_sem.at[index])
        copy.start()
        loads[name] = copy

    load("q", q_hbm, qv, 0)
    for i in range(OWN_ROWS):
        load(("cache", i), cache_hbm.at[i], cv.at[i], 1 + i)
    load("uv", uv_hbm, uv, 5)
    load("out_w", out_w_hbm, out_w, 6)
    load("res", residual_hbm.at[own_lanes], res, 7)
    load("gate", gate_hbm, gate_w, 8)
    load("up", up_hbm, up_w, 9)
    load("down", down_hbm, down_w, 10)

    barrier = pltpu.get_barrier_semaphore()
    peers = [me.sibling()]
    for step in (1, 2, 3):
        peers += [me.first_peer(0, step), me.first_peer(1, step), me.tp_peer(step)]
    for peer in peers:
        pl.semaphore_signal(barrier, inc=1, device_id=peer, device_id_type=MESH)
    pl.semaphore_wait(barrier, len(peers))

    a2a = []
    loads["q"].wait()
    for i in range(OWN_ROWS):
        loads[("cache", i)].wait()
        scores = nt_dot(qv[i], cv[i]) * score_scale
        usable = lax.broadcasted_iota(jnp.int32, scores.shape, 1) < lengths[i]
        peak = jnp.max(jnp.where(usable, scores, -1e30), axis=1, keepdims=True)
        soft = jnp.where(usable, jnp.exp(scores - peak), 0.0)
        total = jnp.sum(soft, axis=1, keepdims=True)
        summed = jnp.dot(soft.astype(BF16), cv[i, :, :LAT], preferred_element_type=F32)
        ctx[i] = (summed / total).astype(BF16)
        for step in (2, 1, 3):
            peer_y = lax.rem(y + step, 4)
            copy = remote(
                ctx.at[i, pl.ds(pl.multiple_of(peer_y * OWN_HEADS, OWN_HEADS), OWN_HEADS)],
                by_head.at[y * OWN_ROWS + i],
                a2a_send.at[i, step - 1],
                a2a_recv.at[i, step - 1],
                me.tp_peer(step),
            )
            copy.start()
            a2a.append(copy)
        by_head[y * OWN_ROWS + i] = ctx[i, pl.ds(pl.multiple_of(y * OWN_HEADS, OWN_HEADS), OWN_HEADS), :]
    for i in range(OWN_ROWS):
        for step in (1, 2, 3):
            source = lax.rem(y + 4 - step, 4)
            remote(
                ctx.at[i, pl.ds(0, OWN_HEADS)],
                by_head.at[source * OWN_ROWS + i],
                a2a_send.at[i, step - 1],
                a2a_recv.at[i, step - 1],
                me.tp_peer(step),
            ).wait_recv()

    loads["uv"].wait()
    for part_of in range(LAT // 128):
        piece = by_head[:, :, pl.ds(part_of * 128, 128)]
        by_head_f[part_of] = piece.astype(F32).reshape(DP_ROWS * OWN_HEADS, 128)
    own_rows = pl.ds(pl.multiple_of(d * DP_ROWS, DP_ROWS), DP_ROWS)
    for h in range(OWN_HEADS):
        picked = jnp.concatenate(
            [
                by_head_f[part_of, pl.ds(h, DP_ROWS, stride=OWN_HEADS), :]
                for part_of in range(LAT // 128)
            ],
            axis=1,
        ).astype(BF16)
        heads_all[own_rows, pl.ds(h * VHEAD, VHEAD)] = jnp.dot(
            picked, uv[h], preferred_element_type=F32
        ).astype(BF16)

    def head_block(dp, half):
        return heads_all.at[
            pl.ds(pl.multiple_of(dp * DP_ROWS, DP_ROWS), DP_ROWS), pl.ds(half * (INNER // 2), INNER // 2)
        ]

    ag = gather_plane(me, head_block, ag_send, ag_recv, ag_sib_send, ag_sib_recv)

    loads["out_w"].wait()
    part[...] = jnp.zeros_like(part)

    def out_step(k, carry):
        at = pl.ds(pl.multiple_of(k * 512, 512), 512)
        part[...] += jnp.dot(heads_all[:, at], out_w[at, :], preferred_element_type=F32)
        return carry

    lax.fori_loop(0, INNER // 512, out_step, 0)
    part_b[...] = part[...].astype(BF16)
    rs = []
    for step in (2, 1, 3):
        peer_y = lax.rem(y + step, 4)
        copy = remote(
            part_b.at[pl.ds(pl.multiple_of(peer_y * TP_ROWS, TP_ROWS), TP_ROWS)],
            part_r.at[step - 1],
            rs_send.at[step - 1],
            rs_recv.at[step - 1],
            me.tp_peer(step),
        )
        copy.start()
        rs.append(copy)

    loads["gate"].wait()
    loads["up"].wait()

    def gain_step(i, carry):
        at = pl.ds(pl.multiple_of(i * 128, 128), 128)
        column = jnp.broadcast_to(gain[pl.ds(i, 1), :], (128, 128)).T
        wide = jnp.concatenate([column, column], axis=1)
        gate_w[at, :] = (gate_w[at, :].astype(F32) * wide).astype(BF16)
        up_w[at, :] = (up_w[at, :].astype(F32) * wide).astype(BF16)
        return carry

    lax.fori_loop(0, D // 128, gain_step, 0)

    mine = jnp.sum(jnp.where(routes[...] == d, route_weights[...], 0.0), axis=1, keepdims=True)
    weight_row[...] = jnp.broadcast_to(mine, (ROWS, 128)).T[:8, :]

    loads["res"].wait()
    for copy in rs:
        copy.wait_recv()
    total = res[...].astype(F32) + part[own_lanes, :]
    for step in (1, 2, 3):
        total = total + part_r[step - 1].astype(F32)
    hidden = total.astype(BF16).astype(F32)
    hid[...] = hidden
    turned = jnp.concatenate([hidden, jnp.zeros((TP_ROWS, 256 - COLS), F32)], axis=1).T
    own_cols = pl.ds(pl.multiple_of(d * COLS, 16), COLS)
    hid_t[own_cols, own_lanes] = turned[:COLS].astype(BF16)

    hy = []
    for step in (2, 1, 3):
        ref = hid_t.at[own_cols, own_lanes]
        copy = remote(ref, ref, hy_send.at[step - 1], hy_recv.at[step - 1], me.tp_peer(step))
        copy.start()
        hy.append(copy)
    for step in (1, 2, 3):
        source = lax.rem(y + 4 - step, 4)
        ref = hid_t.at[own_cols, pl.ds(pl.multiple_of(source * TP_ROWS, TP_ROWS), TP_ROWS)]
        remote(ref, ref, hy_send.at[step - 1], hy_recv.at[step - 1], me.tp_peer(step)).wait_recv()

    def hidden_block(dp, half):
        return hid_t.at[pl.ds(pl.multiple_of(dp * COLS + half * HALF, 16), HALF), :]

    ah = gather_plane(me, hidden_block, ah_send, ah_recv, ah_sib_send, ah_sib_recv)

    gate_acc[...] = jnp.zeros_like(gate_acc)
    up_acc[...] = jnp.zeros_like(up_acc)

    def expert_step(k, squares):
        at = pl.ds(pl.multiple_of(k * 1024, 1024), 1024)
        rows = hid_t[at, :]
        gate_acc[...] += tn_dot(gate_w[at, :], rows)
        up_acc[...] += tn_dot(up_w[at, :], rows)
        wide = rows.astype(F32)
        return squares + jnp.sum((wide * wide).reshape(128, 8, ROWS), axis=0)

    squares = lax.fori_loop(0, D // 1024, expert_step, jnp.zeros((8, ROWS), F32))
    inverse_rms = lax.rsqrt(jnp.sum(squares, axis=0, keepdims=True) * (1.0 / D) + epsilon)
    gate_proj = gate_acc[...] * inverse_rms
    up_proj = up_acc[...] * inverse_rms
    silu = gate_proj / (1.0 + jnp.exp(-gate_proj))
    act[...] = (silu * up_proj * weight_row[0:1, :]).astype(BF16)

    loads["down"].wait()

    def down_step(k, carry):
        at = pl.ds(pl.multiple_of(k * 256, 256), 256)
        contrib[at, :] = tn_dot(down_w[:, at], act[...]).astype(BF16)
        return carry

    lax.fori_loop(0, D // 256, down_step, 0)

    def share(half, j, k, c):
        dp = me.block(half, j, k, c)
        return contrib.at[pl.ds(pl.multiple_of(dp * COLS + half * HALF, 16), HALF), :]

    back = []

    def start(copy):
        copy.start()
        back.append(copy)

    for k in (2, 1, 3, 0):
        for j in ORDER:
            for half in range(2):
                start(remote(
                    share(half, j, k, 1 - me.c), from_sib.at[half, j * 4 + k],
                    sib_send.at[half, j * 4 + k], sib_recv.at[half, j * 4 + k], me.sibling(),
                ))

    def with_sibling(half, j, k):
        remote(
            share(half, j, k, me.c), from_sib.at[half, j * 4 + k],
            sib_send.at[half, j * 4 + k], sib_recv.at[half, j * 4 + k], me.sibling(),
        ).wait_recv()
        return share(half, j, k, me.c)[...].astype(F32) + from_sib[half, j * 4 + k].astype(F32)

    for j in ORDER:
        for half in range(2):
            ref = share(half, j, 2, me.c)
            ref[...] = with_sibling(half, j, 2).astype(BF16)
            step = 1 if j in RIGHT else 3
            start(remote(
                ref, pass_r.at[half, j], pass_send.at[half, j], pass_recv.at[half, j],
                me.second_peer(half, step),
            ))
    for j in (1, 0, 3, 2):
        for half in range(2):
            for k in (1, 3) if j in LEFT else (3, 1):
                ref = share(half, j, k, me.c)
                value = with_sibling(half, j, k)
                if (j in RIGHT) == (k == 1):
                    remote(
                        ref, pass_r.at[half, j], pass_send.at[half, j], pass_recv.at[half, j],
                        me.sibling(),
                    ).wait_recv()
                    value = value + pass_r[half, j].astype(F32)
                ref[...] = value.astype(BF16)
                slot = j * 2 + (0 if k == 1 else 1)
                start(remote(
                    ref, ring_r.at[half, slot], ring_send.at[half, slot], ring_recv.at[half, slot],
                    me.second_peer(half, k),
                ))
    for j in (1, 3, 2, 0):
        for half in range(2):
            ref = share(half, j, 0, me.c)
            value = with_sibling(half, j, 0)
            for slot in (j * 2, j * 2 + 1):
                remote(
                    ref, ring_r.at[half, slot], ring_send.at[half, slot], ring_recv.at[half, slot],
                    me.sibling(),
                ).wait_recv()
                value = value + ring_r[half, slot].astype(F32)
            if j == 0:
                plane_sum[pl.ds(half * HALF, HALF), :] = value
            else:
                ref[...] = value.astype(BF16)
                start(remote(
                    ref, line_r.at[half, j - 1], line_send.at[half, j - 1], line_recv.at[half, j - 1],
                    me.first_peer(half, j),
                ))
    for half in range(2):
        at = pl.ds(half * HALF, HALF)
        value = plane_sum[at, :]
        for j in (1, 2, 3):
            remote(
                share(half, j, 0, me.c), line_r.at[half, j - 1], line_send.at[half, j - 1],
                line_recv.at[half, j - 1], me.sibling(),
            ).wait_recv()
            value = value + line_r[half, j - 1].astype(F32)
        plane_sum[at, :] = value
        plane_sum_b[at, :] = value.astype(BF16)
    for step in (2, 1, 3):
        peer_y = lax.rem(y + step, 4)
        start(remote(
            plane_sum_b.at[:, pl.ds(pl.multiple_of(peer_y * TP_ROWS, TP_ROWS), TP_ROWS)],
            tp_r.at[step - 1], tp_send.at[step - 1], tp_recv.at[step - 1], me.tp_peer(step),
        ))
    moe = plane_sum[:, own_lanes]
    for step in (1, 2, 3):
        remote(
            plane_sum_b.at[:, own_lanes], tp_r.at[step - 1], tp_send.at[step - 1],
            tp_recv.at[step - 1], me.tp_peer(step),
        ).wait_recv()
        moe = moe + tp_r[step - 1].astype(F32)
    moe = jnp.concatenate([moe, jnp.zeros((256 - COLS, TP_ROWS), F32)], axis=0).T
    out[...] = (hid[...] + moe[:, :COLS]).astype(BF16)

    for copy in a2a + ag + rs + hy + ah + back:
        copy.wait_send()


def local(
    queries, latent_cache, lengths, uv_weight, out_weight, residual, norm_gain,
    gate_weight, up_weight, down_weight, routes, route_weights,
):
    anywhere = pl.BlockSpec(memory_space=pl.ANY)
    vmem = pl.BlockSpec(memory_space=pltpu.VMEM)
    smem = pl.BlockSpec(memory_space=pltpu.SMEM)
    dma = pltpu.SemaphoreType.DMA
    scratch = [
        pltpu.VMEM((OWN_ROWS, HEADS, KEY), BF16),
        pltpu.VMEM((OWN_ROWS, CTX, KEY), BF16),
        pltpu.VMEM((OWN_HEADS, LAT, VHEAD), BF16),
        pltpu.VMEM((INNER, COLS), BF16),
        pltpu.VMEM((TP_ROWS, COLS), BF16),
        pltpu.VMEM((D, UNITS), BF16),
        pltpu.VMEM((D, UNITS), BF16),
        pltpu.VMEM((UNITS, D), BF16),
        pltpu.VMEM((OWN_ROWS, HEADS, LAT), BF16),
        pltpu.VMEM((DP_ROWS, OWN_HEADS, LAT), BF16),
        pltpu.VMEM((LAT // 128, DP_ROWS * OWN_HEADS, 128), F32),
        pltpu.VMEM((ROWS, INNER), BF16),
        pltpu.VMEM((ROWS, COLS), F32),
        pltpu.VMEM((ROWS, COLS), BF16),
        pltpu.VMEM((3, TP_ROWS, COLS), BF16),
        pltpu.VMEM((TP_ROWS, COLS), F32),
        pltpu.VMEM((D, ROWS), BF16),
        pltpu.VMEM((UNITS, ROWS), F32),
        pltpu.VMEM((UNITS, ROWS), F32),
        pltpu.VMEM((UNITS, ROWS), BF16),
        pltpu.VMEM((D, ROWS), BF16),
        pltpu.VMEM((2, 16, HALF, ROWS), BF16),
        pltpu.VMEM((2, 4, HALF, ROWS), BF16),
        pltpu.VMEM((2, 8, HALF, ROWS), BF16),
        pltpu.VMEM((2, 3, HALF, ROWS), BF16),
        pltpu.VMEM((COLS, ROWS), F32),
        pltpu.VMEM((COLS, ROWS), BF16),
        pltpu.VMEM((3, COLS, TP_ROWS), BF16),
        pltpu.VMEM((8, ROWS), F32),
        dma((11,)),
        dma((4, 3)), dma((4, 3)),
        dma((2, 15)), dma((2, 16)), dma((2, 16)), dma((2, 16)),
        dma((3,)), dma((3,)),
        dma((3,)), dma((3,)),
        dma((2, 15)), dma((2, 16)), dma((2, 16)), dma((2, 16)),
        dma((2, 16)), dma((2, 16)),
        dma((2, 4)), dma((2, 4)),
        dma((2, 8)), dma((2, 8)),
        dma((2, 3)), dma((2, 3)),
        dma((3,)), dma((3,)),
    ]
    return pl.pallas_call(
        kernel,
        out_shape=jax.ShapeDtypeStruct((TP_ROWS, COLS), BF16),
        in_specs=[smem] + [anywhere] * 5 + [vmem] + [anywhere] * 3 + [vmem] * 2,
        out_specs=vmem,
        scratch_shapes=scratch,
        compiler_params=pltpu.CompilerParams(
            collective_id=0, has_side_effects=True, vmem_limit_bytes=62 * 1024 * 1024
        ),
        name="decode_step",
    )(
        lengths, queries, latent_cache, uv_weight, out_weight, residual,
        norm_gain.reshape(D // 128, 128),
        gate_weight[0], up_weight[0], down_weight[0], routes, route_weights,
    )


def solution(mesh):
    placed = (
        P(("dp", "tp"), None, None),
        P(("dp", "tp"), None, None),
        P(("dp", "tp")),
        P("tp", None, None),
        P("tp", "dp"),
        P(None, "dp"),
        P(),
        P("dp", None, "tp"),
        P("dp", None, "tp"),
        P("dp", "tp", None),
        P(),
        P(),
    )
    return jax.shard_map(
        local, mesh=mesh, in_specs=placed, out_specs=P("tp", "dp"), check_vma=False
    )
```

time: 353 us -> 138 us (0.39)
  waiting for transfers between devices: 176 us -> 0 us
  Pallas kernels: 0 us -> 117 us
  blocking collectives: 83 us -> 0 us
  matrix products: 50.3 us -> 0 us
  between operations: 13.3 us -> 0.01 us
  other arithmetic: 11.7 us -> 0 us
  local copies, waits for them, and re-layouts: 10.7 us -> 20.3 us
  starting transfers between devices: 7.74 us -> 0 us
    pallas_call x0 -> x1, Pallas kernels: none -> 117 us  [local(): pl.pallas_call(kernel, out_shape=jax.ShapeDtypeStruct((TP_ROWS, COLS), BF...]
    all_to_all x2 -> x0, blocking collectives: 83 us -> none  [the longest x1 69.2 us: local(): lax.all_to_all(partial_value, 'dp', split_axis=1, concat_axis=0, tiled=True)]
    all_to_all x1 -> x0, waiting for transfers between devices: 68.4 us -> none  [local(): lax.all_to_all(outgoing, 'dp', split_axis=0, concat_axis=1, tiled=True)]
    all_gather x1 -> x0, waiting for transfers between devices: 46.7 us -> none  [local(): lax.all_gather(head_out, 'dp', axis=0, tiled=True)]
    dot_general x9 -> x0, matrix products: 43.7 us -> none  [the longest x1 16.8 us: local(): jnp.einsum('esr,esd->rd', combiner, returned.astype(jnp.float32).reshape(...]
    psum x1 -> x0, waiting for transfers between devices: 41.5 us -> none  [local(): attn_full = lax.psum(attn_part, 'tp')]
    reduce_scatter x1 -> x0, waiting for transfers between devices: 19 us -> none  [local(): moe_rows = lax.psum_scatter(moe_part, 'tp', scatter_dimension=0, tiled=True)]
    unnamed x16 -> x6, local copies, waits for them, and re-layouts: 0.84 us -> 18.7 us
  transfers between devices with their start and end apart: 4 -> 0, of which waited for: 4 -> 0; matrix products, arithmetic and copies ran while one was open for 0% -> 0% of each run, Pallas kernels for 0% -> 0%
where the time goes in v1:
time: 138 us; the launch traced here: 137 us
  Pallas kernels  117 us (85%)
  local copies, waits for them, and re-layouts  20.3 us (15%)
    pallas_call x1, Pallas kernels, local(): pl.pallas_call(kernel, out_shape=jax.ShapeDtypeStruct((TP_ROWS, COLS), BF...  117 us
    unnamed x6, local copies, waits for them, and re-layouts  18.7 us

profile of v1, /device:TPU:0, one launch (start us, length us, event | category | flops | bytes accessed | tf_op | source)
XLA Modules:
  0.0 137.2 jit_solution(6742953924330126404)
XLA Ops:
  0.0 1.8 %copy.16.residual_hbm = bf16[512,224]{1,0:T(8,128)(2,1)} copy(bf16[512,224]{0,1:T(8,128)(2,1)} %param.17) | data formatting | bytes 458752 | tf_op args[5]
  1.8 1.6 %copy.17.routes = s32[512,8]{1,0:T(8,128)} copy(s32[512,8]{0,1:T(8,128)} %param.22) | data formatting | bytes 32768 | tf_op args[10]
  3.4 1.6 %copy.18.route_weights = f32[512,8]{1,0:T(8,128)} copy(f32[512,8]{0,1:T(8,128)} %param.23) | data formatting | bytes 32768 | tf_op args[11]
  4.9 2.1 %copy.13.q_hbm = bf16[4,128,576]{2,1,0:T(8,128)(2,1)} copy(bf16[4,128,576]{1,2,0:T(8,128)(2,1)} %param.12) | data formatting | bytes 1179648 | tf_op args[0]
  7.1 4.0 %copy.15.out_w_hbm = bf16[4096,224]{1,0:T(8,128)(2,1)} copy(bf16[4096,224]{0,1:T(8,128)(2,1)} %param.16) | data formatting | bytes 3670016 | tf_op args[4]
  11.1 7.7 %copy.14.cache_hbm = bf16[4,1024,576]{2,1,0:T(8,128)(2,1)} copy(bf16[4,1024,576]{1,2,0:T(8,128)(2,1)} %param.13) | data formatting | bytes 9437184 | tf_op args[1]
  18.7 116.9 %decode_step.1 = bf16[128,224]{1,0:T(8,128)(2,1)} custom-call(s32[4]{0:T(128)} %lengths.1, bf16[4,128,576]{2,1,0:T(8,128)(2,1)} %copy.13.q_hbm, bf16[4,1024,576]{2,1,0:T(8,128)(2,1)} %copy.14.cache_hbm, bf16[32,512,128]{2,1,0:T(8,128)(2,1)} %uv_hbm.1, bf16[4096,224]{1,0:T(8,128)(2,1)} %copy.15.out_w_hbm, bf16[512,224]{1,0:T(8,128)(2,1)} %copy.16.residual_hbm, ...), custom_call_target="tpu_custom_call" | custom-call | tf_op jit(solution)/shard_map/decode_step/pallas_call | solution.py:504
  135.6 1.6 %copy.19 = bf16[128,224]{0,1:T(8,128)(2,1)} copy(bf16[128,224]{1,0:T(8,128)(2,1)} %decode_step.1) | data formatting | bytes 114688 | tf_op jit(solution)/shard_map/decode_step/pallas_call | solution.py:504

commit v2 on v1

v2 whole, which is shorter than its diff:
```python
import functools

import jax
import jax.numpy as jnp
from jax import lax
from jax.experimental import pallas as pl
from jax.experimental.pallas import tpu as pltpu
from jax.sharding import PartitionSpec as P

F32 = jnp.float32
BF16 = jnp.bfloat16
MESH = pl.DeviceIdType.MESH

LAT = 512
KEY = 576
CTX = 1024
HEADS = 128
OWN_HEADS = 32
VHEAD = 128
ROWS = 512
OWN_ROWS = 4
DP_ROWS = 16
TP_ROWS = 128
D = 7168
COLS = 224
PART_A = 96
PART_B = 128
INNER = 4096
UNITS = 256
DP = 32

score_scale = 192.0 ** (-0.5)
epsilon = 1e-06

RIGHT = (0, 2)
LEFT = (1, 3)
ORDER = (0, 1, 3, 2)


def tn_dot(a, b):
    return lax.dot_general(a, b, (((0,), (0,)), ((), ())), preferred_element_type=F32)


def nt_dot(a, b):
    return lax.dot_general(a, b, (((1,), (1,)), ((), ())), preferred_element_type=F32)


class Place:
    def __init__(self):
        dp = lax.axis_index("dp")
        self.y = lax.axis_index("tp")
        self.d = dp
        self.c = lax.rem(dp, 2)
        self.x = lax.rem(dp // 2, 4)
        self.z = dp // 8

    def device(self, z=None, x=None, c=None, y=None):
        z = self.z if z is None else z
        x = self.x if x is None else x
        c = self.c if c is None else c
        y = self.y if y is None else y
        return ((z * 4 + x) * 2 + c, y)

    def sibling(self):
        return self.device(c=1 - self.c)

    def tp_peer(self, step):
        return self.device(y=lax.rem(self.y + step, 4))

    def first(self, half):
        return self.x if half == 0 else self.z

    def second(self, half):
        return self.z if half == 0 else self.x

    def first_peer(self, half, step):
        if half == 0:
            return self.device(x=lax.rem(self.x + step, 4))
        return self.device(z=lax.rem(self.z + step, 4))

    def second_peer(self, half, step):
        return self.first_peer(1 - half, step)

    def lanes(self, step):
        at = lax.rem(self.y + step, 4) * TP_ROWS
        return pl.ds(pl.multiple_of(at, TP_ROWS), TP_ROWS)

    def at(self, dz, dx, c):
        return (lax.rem(self.z + dz, 4) * 4 + lax.rem(self.x + dx, 4)) * 2 + c

    def block(self, half, j, k, c):
        a = lax.rem(self.first(half) + j, 4)
        b = lax.rem(self.second(half) + k, 4)
        z, x = (b, a) if half == 0 else (a, b)
        return (z * 4 + x) * 2 + c


def remote(src, dst, send, recv, device):
    return pltpu.make_async_remote_copy(
        src_ref=src, dst_ref=dst, send_sem=send, recv_sem=recv, device_id=device, device_id_type=MESH
    )


def rows_of(dp, offset, count):
    return pl.ds(pl.multiple_of(dp * COLS + offset, 16), count)


def gather_plane(me, blk, start, sems, landed):
    send_sem, recv_sem = sems
    count = [0, 0]

    def ref_of(half, j, k):
        return blk(half, me.block(half, j, k, me.c))

    def send(half, j, k, device, rj, rk):
        ref = ref_of(half, j, k)
        start(remote(
            ref, ref, send_sem.at[half, count[half]], recv_sem.at[half, rj * 4 + rk], device
        ))
        count[half] += 1

    def arrived(half, j, k):
        ref = ref_of(half, j, k)
        remote(
            ref, ref, send_sem.at[half, 0], recv_sem.at[half, j * 4 + k], me.sibling()
        ).wait_recv()

    def second_axis(half, j):
        send(half, j, 0, me.second_peer(half, 1), j, 3)
        send(half, j, 0, me.second_peer(half, 3), j, 1)

    for half in range(2):
        send(half, 0, 0, me.first_peer(half, 1), 3, 0)
        send(half, 0, 0, me.first_peer(half, 3), 1, 0)
    for half in range(2):
        second_axis(half, 0)
    for half in range(2):
        landed(half, 0, 0)
    yield
    for half in range(2):
        arrived(half, 1, 0)
        arrived(half, 3, 0)
        send(half, 3 - 2 * me.c, 0, me.first_peer(half, 1 + 2 * me.c), 2, 0)
    for half in range(2):
        second_axis(half, 1)
        second_axis(half, 3)
    for half in range(2):
        landed(half, 1, 0)
        landed(half, 3, 0)
    yield

    def second_arrivals(j):
        for half in range(2):
            arrived(half, j, 3)
            if j in RIGHT:
                send(half, j, 3, me.second_peer(half, 1), j, 2)
            arrived(half, j, 1)
            if j in LEFT:
                send(half, j, 1, me.second_peer(half, 3), j, 2)
        for half in range(2):
            landed(half, j, 3)
            landed(half, j, 1)

    second_arrivals(0)
    yield
    for half in range(2):
        arrived(half, 2, 0)
        second_axis(half, 2)
    for half in range(2):
        landed(half, 2, 0)
    yield
    for j in (1, 3, 2):
        second_arrivals(j)
        yield
    for j in ORDER:
        for half in range(2):
            arrived(half, j, 2)
            landed(half, j, 2)
        yield


def scatter_plane(me, own, touch, finish, start, bufs, sems):
    pass_r, ring_r, line_r = bufs
    pass_send, pass_recv, ring_send, ring_recv, line_send, line_recv = sems

    def far(half, j, step):
        return remote(
            own(half, j, 2), pass_r.at[half, j], pass_send.at[half, j], pass_recv.at[half, j],
            me.second_peer(half, step),
        )

    def near(half, j, k):
        slot = j * 2 + (0 if k == 1 else 1)
        return remote(
            own(half, j, k), ring_r.at[half, slot], ring_send.at[half, slot],
            ring_recv.at[half, slot], me.second_peer(half, k),
        )

    def line(half, j, slot, step):
        return remote(
            own(half, j, 0), line_r.at[half, slot], line_send.at[half, slot],
            line_recv.at[half, slot], me.first_peer(half, step),
        )

    for j in ORDER:
        for half in range(2):
            own(half, j, 2)[...] = touch(half, j, 2).astype(BF16)
            start(far(half, j, 1 if j in RIGHT else 3))
        yield
    for j in ORDER:
        for half in range(2):
            for k in (1, 3) if j in LEFT else (3, 1):
                value = touch(half, j, k)
                if (j in RIGHT) == (k == 1):
                    far(half, j, 1).wait_recv()
                    value = value + pass_r[half, j].astype(F32)
                own(half, j, k)[...] = value.astype(BF16)
                start(near(half, j, k))
        yield

    def gathered(half, j):
        value = touch(half, j, 0)
        for k in (1, 3):
            near(half, j, k).wait_recv()
            value = value + ring_r[half, j * 2 + (0 if k == 1 else 1)].astype(F32)
        return value

    straight, added = 3 - 2 * me.c, 1 + 2 * me.c
    for half in range(2):
        own(half, 2, 0)[...] = gathered(half, 2).astype(BF16)
        start(line(half, 2, 2, added))
    yield
    for half in range(2):
        for j in (1, 3):
            own(half, j, 0)[...] = gathered(half, j).astype(BF16)
        start(line(half, straight, 0, straight))
    yield
    for half in range(2):
        line(half, 2, 2, added).wait_recv()
        ref = own(half, added, 0)
        ref[...] = (ref[...].astype(F32) + line_r[half, 2].astype(F32)).astype(BF16)
        start(line(half, added, 1, added))
    yield
    for half in range(2):
        value = gathered(half, 0)
        for slot in range(2):
            line(half, 0, slot, 1).wait_recv()
            value = value + line_r[half, slot].astype(F32)
        finish(half, value)
    yield


def kernel(
    lengths, q_hbm, cache_hbm, uv_hbm, out_w_hbm, residual_hbm, gain, gate_hbm, up_hbm, down_hbm,
    routes, route_weights, out,
    qv, cv, uv, out_w, res, down_w, gate_up_t, down_t,
    ctx, by_head, by_head_f, heads_all, part, part_b, part_r, hid, hid_t, gate_up,
    act, contrib, from_sib, plane_sum, plane_sum_b, tp_r, weight_row,
    b_pass, b_ring, b_line, a_pass, a_ring, a_line, a_sum, ya_pass, ya_ring,
    load_sem, a2a_send, a2a_recv, ag_send, ag_recv, ag_sib_send, ag_sib_recv,
    rs_send, rs_recv, hy_send, hy_recv,
    ga_send, ga_recv, gy_send, gy_recv, ga_sib_send, ga_sib_recv,
    gb_send, gb_recv, gb_sib_send, gb_sib_recv,
    sib_send, sib_recv, yp_send, yp_recv, yr_send, yr_recv,
    ap_send, ap_recv, ar_send, ar_recv, al_send, al_recv,
    bp_send, bp_recv, br_send, br_recv, bl_send, bl_recv,
    tp_send, tp_recv,
):
    me = Place()
    y, d = me.y, me.d
    own_lanes = pl.ds(pl.multiple_of(y * TP_ROWS, TP_ROWS), TP_ROWS)

    loads = {}
    sent = []

    def load(name, src, dst, index):
        copy = pltpu.make_async_copy(src, dst, load_sem.at[index])
        copy.start()
        loads[name] = copy

    def ready(name):
        loads.pop(name).wait()

    def start(copy):
        copy.start()
        sent.append(copy)

    load("q", q_hbm, qv, 0)
    for i in range(OWN_ROWS):
        load(("cache", i), cache_hbm.at[i], cv.at[i], 1 + i)

    barrier = pltpu.get_barrier_semaphore()
    peers = [me.sibling()]
    for step in (1, 2, 3):
        peers += [me.first_peer(0, step), me.first_peer(1, step), me.tp_peer(step)]
    for peer in peers:
        pl.semaphore_signal(barrier, inc=1, device_id=peer, device_id_type=MESH)
    pl.semaphore_wait(barrier, len(peers))

    ready("q")
    for i in range(OWN_ROWS):
        ready(("cache", i))
        if i == 1:
            load("uv", uv_hbm, uv, 5)
            load("out_w", out_w_hbm, out_w, 6)
            load("res", residual_hbm.at[:, own_lanes], res, 7)
        if i == 2:
            load("gate", gate_hbm, contrib.at[:, pl.ds(0, UNITS)], 8)
            load("up", up_hbm, contrib.at[:, pl.ds(UNITS, UNITS)], 9)
            load("down", down_hbm, down_w, 10)
        scores = tn_dot(qv[i], cv[i]) * score_scale
        usable = lax.broadcasted_iota(jnp.int32, scores.shape, 1) < lengths[i]
        peak = jnp.max(jnp.where(usable, scores, -1e30), axis=1, keepdims=True)
        soft = jnp.where(usable, jnp.exp(scores - peak), 0.0)
        total = jnp.sum(soft, axis=1, keepdims=True)
        summed = nt_dot(soft.astype(BF16), cv[i, :LAT, :])
        ctx[i] = (summed / total).astype(BF16)
        for step in (2, 1, 3):
            peer_y = lax.rem(y + step, 4)
            start(remote(
                ctx.at[i, pl.ds(pl.multiple_of(peer_y * OWN_HEADS, OWN_HEADS), OWN_HEADS)],
                by_head.at[y * OWN_ROWS + i],
                a2a_send.at[i, step - 1],
                a2a_recv.at[i, step - 1],
                me.tp_peer(step),
            ))
        by_head[y * OWN_ROWS + i] = ctx[i, pl.ds(pl.multiple_of(y * OWN_HEADS, OWN_HEADS), OWN_HEADS), :]
    for i in range(OWN_ROWS):
        for step in (1, 2, 3):
            source = lax.rem(y + 4 - step, 4)
            remote(
                ctx.at[i, pl.ds(0, OWN_HEADS)],
                by_head.at[source * OWN_ROWS + i],
                a2a_send.at[i, step - 1],
                a2a_recv.at[i, step - 1],
                me.tp_peer(step),
            ).wait_recv()

    ready("uv")
    for part_of in range(LAT // 128):
        piece = by_head[:, :, pl.ds(part_of * 128, 128)]
        by_head_f[part_of] = piece.astype(F32).reshape(DP_ROWS * OWN_HEADS, 128)
    own_rows = pl.ds(pl.multiple_of(d * DP_ROWS, DP_ROWS), DP_ROWS)
    for h in range(OWN_HEADS):
        picked = jnp.concatenate(
            [
                by_head_f[part_of, pl.ds(h, DP_ROWS, stride=OWN_HEADS), :]
                for part_of in range(LAT // 128)
            ],
            axis=1,
        ).astype(BF16)
        heads_all[own_rows, pl.ds(h * VHEAD, VHEAD)] = jnp.dot(
            picked, uv[h], preferred_element_type=F32
        ).astype(BF16)

    def head_block(half, dp):
        return heads_all.at[
            pl.ds(pl.multiple_of(dp * DP_ROWS, DP_ROWS), DP_ROWS), pl.ds(half * (INNER // 2), INNER // 2)
        ]

    def head_sibling(half, j, k, c):
        ref = head_block(half, me.block(half, j, k, c))
        return remote(
            ref, ref, ag_sib_send.at[half, j * 4 + k], ag_sib_recv.at[half, j * 4 + k], me.sibling()
        )

    def turn_step(i, carry):
        at = pl.ds(pl.multiple_of(i * 128, 128), 128)
        turned = contrib[at, :].astype(F32).T * gain[pl.ds(i, 1), :]
        gate_up_t[:, at] = turned.astype(BF16)
        down_t[at, :] = down_w[:, at].astype(F32).T.astype(BF16)
        return carry

    turned_to = 0
    for step in gather_plane(
        me, head_block, start, (ag_send, ag_recv), lambda *at: start(head_sibling(*at, me.c))
    ):
        if turned_to == 0:
            ready("gate")
            ready("up")
            ready("down")
        upto = min(turned_to + 7, D // 128)
        lax.fori_loop(turned_to, upto, turn_step, 0)
        turned_to = upto
    for half in range(2):
        for j in range(4):
            for k in range(4):
                head_sibling(half, j, k, 1 - me.c).wait_recv()

    ready("out_w")
    part[...] = jnp.zeros_like(part)

    def out_step(k, carry):
        at = pl.ds(pl.multiple_of(k * 512, 512), 512)
        part[...] += nt_dot(out_w[:, at], heads_all[:, at])
        return carry

    lax.fori_loop(0, INNER // 512, out_step, 0)
    for block in range(4):
        part_b[block] = part[:, block * TP_ROWS : (block + 1) * TP_ROWS].astype(BF16)
    for step in (2, 1, 3):
        start(remote(
            part_b.at[lax.rem(y + step, 4)], part_r.at[step - 1],
            rs_send.at[step - 1], rs_recv.at[step - 1], me.tp_peer(step),
        ))

    weight_row[...] = jnp.sum(
        jnp.where(routes[...] == d, route_weights[...], 0.0), axis=0, keepdims=True
    )

    ready("res")
    total = res[...].astype(F32) + part[:, own_lanes]
    for step in (1, 2, 3):
        remote(
            part_b.at[0], part_r.at[step - 1], rs_send.at[step - 1], rs_recv.at[step - 1],
            me.tp_peer(step),
        ).wait_recv()
        total = total + part_r[step - 1].astype(F32)
    hidden = total.astype(BF16)
    hid[...] = hidden.astype(F32)
    own_cols = pl.ds(pl.multiple_of(d * COLS, 16), COLS)
    hid_t[own_cols, own_lanes] = hidden

    pairs = [(dz, dx) for dz in range(4) for dx in range(4)]

    def a_block(half, dp):
        return hid_t.at[rows_of(dp, half * (PART_A // 2), PART_A // 2), own_lanes]

    def b_block(half, dp):
        return hid_t.at[rows_of(dp, PART_A + half * (PART_B // 2), PART_B // 2), :]

    def pair_of(half, j, k):
        return (k, j) if half == 0 else (j, k)

    def a_tp(pair, slot, lanes, step):
        ref = hid_t.at[rows_of(me.at(*pair, me.c), 0, PART_A), lanes]
        n = pair[0] * 4 + pair[1]
        return remote(ref, ref, gy_send.at[n, slot], gy_recv.at[n, slot], me.tp_peer(step))

    def a_sibling(pair, c):
        ref = hid_t.at[rows_of(me.at(*pair, c), 0, PART_A), :]
        n = pair[0] * 4 + pair[1]
        return remote(ref, ref, ga_sib_send.at[n], ga_sib_recv.at[n], me.sibling())

    a_halves, a_landed = set(), []

    def a_here(half, j, k):
        pair = pair_of(half, j, k)
        if pair in a_halves:
            a_landed.append(pair)
            start(a_tp(pair, 0, me.lanes(0), 1))
            start(a_tp(pair, 1, me.lanes(0), 3))
        a_halves.add(pair)

    a_passed, a_done = [0], [0]

    def a_pass_on(count):
        for pair in a_landed[a_passed[0] : a_passed[0] + count]:
            if sum(pair) % 2 == 0:
                a_tp(pair, 0, me.lanes(3), 1).wait_recv()
                start(a_tp(pair, 2, me.lanes(3), 1))
            else:
                a_tp(pair, 1, me.lanes(1), 3).wait_recv()
                start(a_tp(pair, 2, me.lanes(1), 3))
        a_passed[0] += count

    def a_finish(count):
        for pair in a_landed[a_done[0] : a_done[0] + count]:
            slot, step = (1, 1) if sum(pair) % 2 == 0 else (0, 3)
            a_tp(pair, slot, me.lanes(step), step).wait_recv()
            a_tp(pair, 2, me.lanes(2), 1).wait_recv()
            start(a_sibling(pair, me.c))
        a_done[0] += count

    def b_sibling(half, j, k, c):
        ref = b_block(half, me.block(half, j, k, c))
        return remote(
            ref, ref, gb_sib_send.at[half, j * 4 + k], gb_sib_recv.at[half, j * 4 + k], me.sibling()
        )

    def b_tp(slot, lanes, step):
        ref = hid_t.at[rows_of(d, PART_A, PART_B), lanes]
        return remote(ref, ref, hy_send.at[slot], hy_recv.at[slot], me.tp_peer(step))

    a_plane = gather_plane(me, a_block, start, (ga_send, ga_recv), a_here)
    b_plane = gather_plane(
        me, b_block, start, (gb_send, gb_recv), lambda *at: start(b_sibling(*at, me.c))
    )
    start(b_tp(0, me.lanes(0), 1))
    start(b_tp(1, me.lanes(0), 3))
    next(a_plane)
    b_tp(0, me.lanes(3), 1).wait_recv()
    b_tp(1, me.lanes(1), 1).wait_recv()
    start(b_tp(2, me.lanes(3 - 2 * me.c), 1 + 2 * me.c))
    next(a_plane)
    a_pass_on(1)
    b_tp(2, me.lanes(2), 1).wait_recv()
    next(b_plane)
    for _ in range(5):
        next(a_plane)
    next(b_plane)
    for _ in range(4):
        next(a_plane)
    for _ in range(2):
        next(b_plane)
        a_pass_on(3)
    for _ in range(3):
        next(b_plane)
        a_pass_on(3)
        a_finish(3)
    for _ in range(4):
        next(b_plane)
        a_finish(2)
    a_finish(16 - a_done[0])
    for half in range(2):
        for j in range(4):
            for k in range(4):
                b_sibling(half, j, k, 1 - me.c).wait_recv()
    for pair in pairs:
        a_sibling(pair, 1 - me.c).wait_recv()

    gate_up[...] = jnp.zeros_like(gate_up)

    def expert_step(k, squares):
        at = pl.ds(pl.multiple_of(k * 1024, 1024), 1024)
        rows = hid_t[at, :]
        gate_up[...] += jnp.dot(gate_up_t[:, at], rows, preferred_element_type=F32)
        wide = rows.astype(F32)
        return squares + jnp.sum((wide * wide).reshape(128, 8, ROWS), axis=0)

    squares = lax.fori_loop(0, D // 1024, expert_step, jnp.zeros((8, ROWS), F32))
    inverse_rms = lax.rsqrt(jnp.sum(squares, axis=0, keepdims=True) * (1.0 / D) + epsilon)
    gate_proj = gate_up[:UNITS, :] * inverse_rms
    up_proj = gate_up[UNITS:, :] * inverse_rms
    silu = gate_proj / (1.0 + jnp.exp(-gate_proj))
    act[...] = (silu * up_proj * weight_row[...]).astype(BF16)

    def from_core(pair, c):
        n = pair[0] * 4 + pair[1]
        return remote(
            contrib.at[rows_of(me.at(*pair, c), 0, COLS), :], from_sib.at[n],
            sib_send.at[n], sib_recv.at[n], me.sibling(),
        )

    def compute(pair):
        at = pl.ds(pl.multiple_of(me.at(*pair, 0) * COLS, 16), 2 * COLS)
        contrib[at, :] = jnp.dot(down_t[at, :], act[...], preferred_element_type=F32).astype(BF16)
        start(from_core(pair, 1 - me.c))

    sib_here = set()

    def sibling_here(pair):
        if pair not in sib_here:
            sib_here.add(pair)
            from_core(pair, me.c).wait_recv()

    def ya_far(pair, step):
        n = pair[0] * 4 + pair[1]
        return remote(
            contrib.at[rows_of(me.at(*pair, me.c), 0, PART_A), me.lanes(2)], ya_pass.at[n],
            yp_send.at[n], yp_recv.at[n], me.tp_peer(step),
        )

    def ya_near(pair, step):
        n = pair[0] * 4 + pair[1]
        slot = 0 if step == 1 else 1
        return remote(
            contrib.at[rows_of(me.at(*pair, me.c), 0, PART_A), me.lanes(step)], ya_ring.at[n, slot],
            yr_send.at[n, slot], yr_recv.at[n, slot], me.tp_peer(step),
        )

    def a_first(pair):
        sibling_here(pair)
        at = rows_of(me.at(*pair, me.c), 0, PART_A)
        theirs = from_sib[pair[0] * 4 + pair[1], :PART_A, :]
        contrib[at, :] = (contrib[at, :].astype(F32) + theirs.astype(F32)).astype(BF16)
        far_step = 1 if sum(pair) % 2 == 0 else 3
        start(ya_far(pair, far_step))
        start(ya_near(pair, 4 - far_step))

    def a_second(pair):
        step = 1 if sum(pair) % 2 == 0 else 3
        ya_far(pair, step).wait_recv()
        at = rows_of(me.at(*pair, me.c), 0, PART_A)
        passed = ya_pass[pair[0] * 4 + pair[1]].astype(F32)
        contrib[at, me.lanes(step)] = (contrib[at, me.lanes(step)].astype(F32) + passed).astype(BF16)
        start(ya_near(pair, step))

    def a_third(pair):
        n = pair[0] * 4 + pair[1]
        value = contrib[rows_of(me.at(*pair, me.c), 0, PART_A), own_lanes].astype(F32)
        for step in (1, 3):
            ya_near(pair, step).wait_recv()
            value = value + ya_ring[n, 0 if step == 1 else 1].astype(F32)
        a_sum[n] = value.astype(BF16)

    def a_own(half, j, k):
        a = lax.rem(me.first(half) + j, 4)
        b = lax.rem(me.second(half) + k, 4)
        dz, dx = (k, j) if half == 0 else (j, k)
        return a_sum.at[dz * 4 + dx, pl.ds(half * (PART_A // 2), PART_A // 2), :]

    def a_touch(half, j, k):
        return a_own(half, j, k)[...].astype(F32)

    def a_final(half, value):
        at = pl.ds(half * (PART_A // 2), PART_A // 2)
        out[at, :] = (hid[at, :] + value).astype(BF16)

    def b_own(half, j, k):
        return contrib.at[
            rows_of(me.block(half, j, k, me.c), PART_A + half * (PART_B // 2), PART_B // 2), :
        ]

    def b_touch(half, j, k):
        pair = pair_of(half, j, k)
        sibling_here(pair)
        theirs = from_sib[
            pair[0] * 4 + pair[1], pl.ds(PART_A + half * (PART_B // 2), PART_B // 2), :
        ]
        return b_own(half, j, k)[...].astype(F32) + theirs.astype(F32)

    def b_final(half, value):
        at = pl.ds(half * (PART_B // 2), PART_B // 2)
        plane_sum[at, :] = value
        plane_sum_b[at, :] = value.astype(BF16)

    a_back = scatter_plane(
        me, a_own, a_touch, a_final, start, (a_pass, a_ring, a_line),
        (ap_send, ap_recv, ar_send, ar_recv, al_send, al_recv),
    )
    b_back = scatter_plane(
        me, b_own, b_touch, b_final, start, (b_pass, b_ring, b_line),
        (bp_send, bp_recv, br_send, br_recv, bl_send, bl_recv),
    )
    order = [(2, 2), (2, 0), (0, 2), (2, 1), (1, 2), (2, 3), (3, 2)]
    order += [pair for pair in pairs if pair not in order]
    for n, pair in enumerate(order):
        compute(pair)
        if n >= 8:
            a_first(order[n - 8])
    for n in range(4):
        next(b_back)
        a_first(order[8 + 2 * n])
        a_first(order[9 + 2 * n])
        a_second(order[2 * n])
        a_second(order[2 * n + 1])
    for n in range(4):
        next(b_back)
        a_second(order[8 + 2 * n])
        a_second(order[9 + 2 * n])
        a_third(order[2 * n])
        a_third(order[2 * n + 1])
    for _ in range(2):
        next(b_back)
    for _ in range(4):
        next(a_back)
    for n in range(8, 16):
        a_third(order[n])
    next(b_back)
    for _ in range(4):
        next(a_back)
    next(b_back)

    def b_tp_sum(step):
        return remote(
            plane_sum_b.at[:, me.lanes(step)], tp_r.at[step - 1],
            tp_send.at[step - 1], tp_recv.at[step - 1], me.tp_peer(step),
        )

    for step in (2, 1, 3):
        start(b_tp_sum(step))
    for _ in range(4):
        next(a_back)
    moe = plane_sum[:, own_lanes]
    for step in (1, 2, 3):
        b_tp_sum(step).wait_recv()
        moe = moe + tp_r[step - 1].astype(F32)
    out[PART_A:, :] = (hid[PART_A:, :] + moe).astype(BF16)

    for copy in sent:
        copy.wait_send()


def local(
    queries, latent_cache, lengths, uv_weight, out_weight, residual, norm_gain,
    gate_weight, up_weight, down_weight, routes, route_weights,
):
    anywhere = pl.BlockSpec(memory_space=pl.ANY)
    vmem = pl.BlockSpec(memory_space=pltpu.VMEM)
    smem = pl.BlockSpec(memory_space=pltpu.SMEM)
    dma = pltpu.SemaphoreType.DMA
    scratch = [
        pltpu.VMEM((OWN_ROWS, KEY, HEADS), BF16),
        pltpu.VMEM((OWN_ROWS, KEY, CTX), BF16),
        pltpu.VMEM((OWN_HEADS, LAT, VHEAD), BF16),
        pltpu.VMEM((COLS, INNER), BF16),
        pltpu.VMEM((COLS, TP_ROWS), BF16),
        pltpu.VMEM((UNITS, D), BF16),
        pltpu.VMEM((2 * UNITS, D), BF16),
        pltpu.VMEM((D, UNITS), BF16),
        pltpu.VMEM((OWN_ROWS, HEADS, LAT), BF16),
        pltpu.VMEM((DP_ROWS, OWN_HEADS, LAT), BF16),
        pltpu.VMEM((LAT // 128, DP_ROWS * OWN_HEADS, 128), F32),
        pltpu.VMEM((ROWS, INNER), BF16),
        pltpu.VMEM((COLS, ROWS), F32),
        pltpu.VMEM((4, COLS, TP_ROWS), BF16),
        pltpu.VMEM((3, COLS, TP_ROWS), BF16),
        pltpu.VMEM((COLS, TP_ROWS), F32),
        pltpu.VMEM((D, ROWS), BF16),
        pltpu.VMEM((2 * UNITS, ROWS), F32),
        pltpu.VMEM((UNITS, ROWS), BF16),
        pltpu.VMEM((D, ROWS), BF16),
        pltpu.VMEM((16, COLS, ROWS), BF16),
        pltpu.VMEM((PART_B, ROWS), F32),
        pltpu.VMEM((PART_B, ROWS), BF16),
        pltpu.VMEM((3, PART_B, TP_ROWS), BF16),
        pltpu.VMEM((1, ROWS), F32),
        pltpu.VMEM((2, 4, PART_B // 2, ROWS), BF16),
        pltpu.VMEM((2, 8, PART_B // 2, ROWS), BF16),
        pltpu.VMEM((2, 3, PART_B // 2, ROWS), BF16),
        pltpu.VMEM((2, 4, PART_A // 2, TP_ROWS), BF16),
        pltpu.VMEM((2, 8, PART_A // 2, TP_ROWS), BF16),
        pltpu.VMEM((2, 3, PART_A // 2, TP_ROWS), BF16),
        pltpu.VMEM((16, PART_A, TP_ROWS), BF16),
        pltpu.VMEM((16, PART_A, TP_ROWS), BF16),
        pltpu.VMEM((16, 2, PART_A, TP_ROWS), BF16),
        dma((11,)),
        dma((4, 3)), dma((4, 3)),
        dma((2, 15)), dma((2, 16)), dma((2, 16)), dma((2, 16)),
        dma((3,)), dma((3,)),
        dma((3,)), dma((3,)),
        dma((2, 15)), dma((2, 16)), dma((16, 3)), dma((16, 3)), dma((16,)), dma((16,)),
        dma((2, 15)), dma((2, 16)), dma((2, 16)), dma((2, 16)),
        dma((16,)), dma((16,)), dma((16,)), dma((16,)), dma((16, 2)), dma((16, 2)),
        dma((2, 4)), dma((2, 4)), dma((2, 8)), dma((2, 8)), dma((2, 3)), dma((2, 3)),
        dma((2, 4)), dma((2, 4)), dma((2, 8)), dma((2, 8)), dma((2, 3)), dma((2, 3)),
        dma((3,)), dma((3,)),
    ]
    return pl.pallas_call(
        kernel,
        out_shape=jax.ShapeDtypeStruct((COLS, TP_ROWS), BF16),
        in_specs=[smem] + [anywhere] * 5 + [vmem] + [anywhere] * 3 + [vmem] * 2,
        out_specs=vmem,
        scratch_shapes=scratch,
        compiler_params=pltpu.CompilerParams(
            collective_id=0, has_side_effects=True, vmem_limit_bytes=62 * 1024 * 1024
        ),
        name="decode_step",
    )(
        lengths, jnp.swapaxes(queries, 1, 2), jnp.swapaxes(latent_cache, 1, 2), uv_weight,
        out_weight.T, residual.T, norm_gain.reshape(D // 128, 128),
        gate_weight[0], up_weight[0], down_weight[0], routes.T, route_weights.T,
    ).T


def solution(mesh):
    placed = (
        P(("dp", "tp"), None, None),
        P(("dp", "tp"), None, None),
        P(("dp", "tp")),
        P("tp", None, None),
        P("tp", "dp"),
        P(None, "dp"),
        P(),
        P("dp", None, "tp"),
        P("dp", None, "tp"),
        P("dp", "tp", None),
        P(),
        P(),
    )
    return jax.shard_map(
        local, mesh=mesh, in_specs=placed, out_specs=P("tp", "dp"), check_vma=False
    )
```

time: 138 us -> 115 us (0.83)
  local copies, waits for them, and re-layouts: 20.3 us -> 1.45 us
  Pallas kernels: 117 us -> 113 us
    unnamed x6 -> x1, local copies, waits for them, and re-layouts: 18.7 us -> 1.45 us
    pallas_call x1, Pallas kernels: 117 us -> 113 us  [local(): pl.pallas_call(kernel, out_shape=jax.ShapeDtypeStruct((COLS, TP_ROWS), BF...]
    pallas_call x1 -> x0, local copies, waits for them, and re-layouts: 1.56 us -> none  [local(): pl.pallas_call(kernel, out_shape=jax.ShapeDtypeStruct((TP_ROWS, COLS), BF...]
where the time goes in v2:
time: 115 us
  Pallas kernels  113 us (98%)
  local copies, waits for them, and re-layouts  1.45 us (1%)
    pallas_call x1, Pallas kernels, local(): pl.pallas_call(kernel, out_shape=jax.ShapeDtypeStruct((COLS, TP_ROWS), BF...  113 us

profile of v2, /device:TPU:0, one launch (start us, length us, event | category | flops | bytes accessed | tf_op | source)
XLA Modules:
  0.0 114.6 jit_solution(11893154727390892760)
XLA Ops:
  0.0 113.2 %decode_step.1 = bf16[224,128]{1,0:T(8,128)(2,1)} custom-call(s32[4]{0:T(128)} %lengths.1, bf16[4,576,128]{2,1,0:T(8,128)(2,1)} %bitcast.16, bf16[4,576,1024]{2,1,0:T(8,128)(2,1)} %bitcast.11, bf16[32,512,128]{2,1,0:T(8,128)(2,1)} %uv_hbm.1, bf16[224,4096]{1,0:T(8,128)(2,1)} %bitcast.15, bf16[224,512]{1,0:T(8,128)(2,1)} %bitcast.17, f32[56,128]{1,0:T(8,128)} %bitcast.19, ...), custom_call_target="tpu_custom_call" | custom-call | tf_op jit(solution)/shard_map/decode_step/pallas_call | solution.py:740
  113.2 1.4 %copy.14 = bf16[128,224]{0,1:T(8,128)(2,1)} copy(bf16[128,224]{0,1:T(8,128)(2,1)} %bitcast.18) | data formatting | bytes 114688

commit v3 on v2

--- a/solution.py
+++ b/solution.py
@@ -32,9 +32,10 @@
 score_scale = 192.0 ** (-0.5)
 epsilon = 1e-06
 
-RIGHT = (0, 2)
-LEFT = (1, 3)
-ORDER = (0, 1, 3, 2)
+SUM_A = 64
+SUM_B = 160
+PASSED = 10
+SUM_PASSED = 8
 
 
 def tn_dot(a, b):
@@ -128,40 +129,24 @@
     def second_axis(half, j):
         send(half, j, 0, me.second_peer(half, 1), j, 3)
         send(half, j, 0, me.second_peer(half, 3), j, 1)
+        if j > 1:
+            send(half, j, 0, me.second_peer(half, 2), j, 2)
 
     for half in range(2):
-        send(half, 0, 0, me.first_peer(half, 1), 3, 0)
-        send(half, 0, 0, me.first_peer(half, 3), 1, 0)
+        for step in (1, 3, 2):
+            send(half, 0, 0, me.first_peer(half, step), 4 - step, 0)
     for half in range(2):
         second_axis(half, 0)
     for half in range(2):
         landed(half, 0, 0)
     yield
-    for half in range(2):
-        arrived(half, 1, 0)
-        arrived(half, 3, 0)
-        send(half, 3 - 2 * me.c, 0, me.first_peer(half, 1 + 2 * me.c), 2, 0)
-    for half in range(2):
-        second_axis(half, 1)
-        second_axis(half, 3)
-    for half in range(2):
-        landed(half, 1, 0)
-        landed(half, 3, 0)
-    yield
-
-    def second_arrivals(j):
-        for half in range(2):
-            arrived(half, j, 3)
-            if j in RIGHT:
-                send(half, j, 3, me.second_peer(half, 1), j, 2)
-            arrived(half, j, 1)
-            if j in LEFT:
-                send(half, j, 1, me.second_peer(half, 3), j, 2)
-        for half in range(2):
-            landed(half, j, 3)
-            landed(half, j, 1)
-
-    second_arrivals(0)
+    for j in (1, 3):
+        for half in range(2):
+            arrived(half, j, 0)
+            second_axis(half, j)
+    for j in (1, 3):
+        for half in range(2):
+            landed(half, j, 0)
     yield
     for half in range(2):
         arrived(half, 2, 0)
@@ -169,83 +154,99 @@
     for half in range(2):
         landed(half, 2, 0)
     yield
-    for j in (1, 3, 2):
-        second_arrivals(j)
+    for j in (0, 1, 3, 2):
+        for half in range(2):
+            arrived(half, j, 3)
+            if j == 0:
+                send(half, j, 3, me.second_peer(half, 1), j, 2)
+            arrived(half, j, 1)
+            if j == 1:
+                send(half, j, 1, me.second_peer(half, 3), j, 2)
+        for half in range(2):
+            landed(half, j, 3)
+            landed(half, j, 1)
         yield
-    for j in ORDER:
+    for j in (0, 1, 3, 2):
         for half in range(2):
             arrived(half, j, 2)
             landed(half, j, 2)
         yield
 
 
-def scatter_plane(me, own, touch, finish, start, bufs, sems):
+def scatter_plane(me, own, touch, finish, start, bufs, sems, passing):
     pass_r, ring_r, line_r = bufs
     pass_send, pass_recv, ring_send, ring_recv, line_send, line_recv = sems
 
-    def far(half, j, step):
-        return remote(
-            own(half, j, 2), pass_r.at[half, j], pass_send.at[half, j], pass_recv.at[half, j],
-            me.second_peer(half, step),
+    def far(half, j):
+        return remote(
+            own(half, j, 2), pass_r.at[half, j - 1], pass_send.at[half, j - 1],
+            pass_recv.at[half, j - 1], me.second_peer(half, 1 if j == 2 else 3),
         )
 
     def near(half, j, k):
-        slot = j * 2 + (0 if k == 1 else 1)
+        slot = j * 3 + k - 1
         return remote(
             own(half, j, k), ring_r.at[half, slot], ring_send.at[half, slot],
             ring_recv.at[half, slot], me.second_peer(half, k),
         )
 
-    def line(half, j, slot, step):
-        return remote(
-            own(half, j, 0), line_r.at[half, slot], line_send.at[half, slot],
-            line_recv.at[half, slot], me.first_peer(half, step),
-        )
-
-    for j in ORDER:
-        for half in range(2):
-            own(half, j, 2)[...] = touch(half, j, 2).astype(BF16)
-            start(far(half, j, 1 if j in RIGHT else 3))
-        yield
-    for j in ORDER:
-        for half in range(2):
-            for k in (1, 3) if j in LEFT else (3, 1):
-                value = touch(half, j, k)
-                if (j in RIGHT) == (k == 1):
-                    far(half, j, 1).wait_recv()
-                    value = value + pass_r[half, j].astype(F32)
-                own(half, j, k)[...] = value.astype(BF16)
-                start(near(half, j, k))
-        yield
+    def line(half, j):
+        return remote(
+            own(half, j, 0), line_r.at[half, j - 1], line_send.at[half, j - 1],
+            line_recv.at[half, j - 1], me.first_peer(half, j),
+        )
+
+    def give(j, k):
+        for half in range(2):
+            own(half, j, k)[...] = touch(half, j, k).astype(BF16)
+            start(near(half, j, k))
+
+    def give_passed(j, k):
+        for half in range(2):
+            value = touch(half, j, k)
+            far(half, j).wait_recv()
+            value = value + pass_r[half, j - 1].astype(F32)
+            own(half, j, k)[...] = value.astype(BF16)
+            start(near(half, j, k))
 
     def gathered(half, j):
         value = touch(half, j, 0)
-        for k in (1, 3):
+        for k in (1, 3, 2):
+            if k == 2 and passing and j in (1, 2):
+                continue
             near(half, j, k).wait_recv()
-            value = value + ring_r[half, j * 2 + (0 if k == 1 else 1)].astype(F32)
+            value = value + ring_r[half, j * 3 + k - 1].astype(F32)
         return value
 
-    straight, added = 3 - 2 * me.c, 1 + 2 * me.c
-    for half in range(2):
-        own(half, 2, 0)[...] = gathered(half, 2).astype(BF16)
-        start(line(half, 2, 2, added))
+    for j in (2, 1):
+        for half in range(2):
+            own(half, j, 2)[...] = touch(half, j, 2).astype(BF16)
+            start(far(half, j) if passing else near(half, j, 2))
+        yield
+    give(2, 3)
+    give(1, 1)
     yield
-    for half in range(2):
-        for j in (1, 3):
+    give(3, 2)
+    give(3, 1)
+    give(3, 3)
+    yield
+    (give_passed if passing else give)(2, 1)
+    (give_passed if passing else give)(1, 3)
+    yield
+    give(0, 2)
+    give(0, 1)
+    give(0, 3)
+    yield
+    for j in (2, 1, 3):
+        for half in range(2):
             own(half, j, 0)[...] = gathered(half, j).astype(BF16)
-        start(line(half, straight, 0, straight))
-    yield
-    for half in range(2):
-        line(half, 2, 2, added).wait_recv()
-        ref = own(half, added, 0)
-        ref[...] = (ref[...].astype(F32) + line_r[half, 2].astype(F32)).astype(BF16)
-        start(line(half, added, 1, added))
-    yield
+            start(line(half, j))
+        yield
     for half in range(2):
         value = gathered(half, 0)
-        for slot in range(2):
-            line(half, 0, slot, 1).wait_recv()
-            value = value + line_r[half, slot].astype(F32)
+        for j in (1, 3, 2):
+            line(half, j).wait_recv()
+            value = value + line_r[half, j - 1].astype(F32)
         finish(half, value)
     yield
 
@@ -295,7 +296,6 @@
         peers += [me.first_peer(0, step), me.first_peer(1, step), me.tp_peer(step)]
     for peer in peers:
         pl.semaphore_signal(barrier, inc=1, device_id=peer, device_id_type=MESH)
-    pl.semaphore_wait(barrier, len(peers))
 
     ready("q")
     for i in range(OWN_ROWS):
@@ -315,16 +315,20 @@
         total = jnp.sum(soft, axis=1, keepdims=True)
         summed = nt_dot(soft.astype(BF16), cv[i, :LAT, :])
         ctx[i] = (summed / total).astype(BF16)
-        for step in (2, 1, 3):
-            peer_y = lax.rem(y + step, 4)
-            start(remote(
-                ctx.at[i, pl.ds(pl.multiple_of(peer_y * OWN_HEADS, OWN_HEADS), OWN_HEADS)],
-                by_head.at[y * OWN_ROWS + i],
-                a2a_send.at[i, step - 1],
-                a2a_recv.at[i, step - 1],
-                me.tp_peer(step),
-            ))
-        by_head[y * OWN_ROWS + i] = ctx[i, pl.ds(pl.multiple_of(y * OWN_HEADS, OWN_HEADS), OWN_HEADS), :]
+        if i < 2:
+            continue
+        if i == 2:
+            pl.semaphore_wait(barrier, len(peers))
+        for row in range(3) if i == 2 else (3,):
+            for step in (2, 1, 3):
+                to = pl.multiple_of(lax.rem(y + step, 4) * OWN_HEADS, OWN_HEADS)
+                start(remote(
+                    ctx.at[row, pl.ds(to, OWN_HEADS)], by_head.at[y * OWN_ROWS + row],
+                    a2a_send.at[row, step - 1], a2a_recv.at[row, step - 1], me.tp_peer(step),
+                ))
+            by_head[y * OWN_ROWS + row] = ctx[
+                row, pl.ds(pl.multiple_of(y * OWN_HEADS, OWN_HEADS), OWN_HEADS), :
+            ]
     for i in range(OWN_ROWS):
         for step in (1, 2, 3):
             source = lax.rem(y + 4 - step, 4)
@@ -450,12 +454,14 @@
             a_landed.append(pair)
             start(a_tp(pair, 0, me.lanes(0), 1))
             start(a_tp(pair, 1, me.lanes(0), 3))
+            if len(a_landed) > PASSED:
+                start(a_tp(pair, 2, me.lanes(0), 2))
         a_halves.add(pair)
 
     a_passed, a_done = [0], [0]
 
     def a_pass_on(count):
-        for pair in a_landed[a_passed[0] : a_passed[0] + count]:
+        for pair in a_landed[a_passed[0] : min(a_passed[0] + count, PASSED)]:
             if sum(pair) % 2 == 0:
                 a_tp(pair, 0, me.lanes(3), 1).wait_recv()
                 start(a_tp(pair, 2, me.lanes(3), 1))
@@ -465,9 +471,11 @@
         a_passed[0] += count
 
     def a_finish(count):
-        for pair in a_landed[a_done[0] : a_done[0] + count]:
-            slot, step = (1, 1) if sum(pair) % 2 == 0 else (0, 3)
-            a_tp(pair, slot, me.lanes(step), step).wait_recv()
+        for n in range(a_done[0], min(a_done[0] + count, 16)):
+            pair = a_landed[n]
+            for slot, step in ((1, 1), (0, 3)):
+                if n >= PASSED or (step == 1) == (sum(pair) % 2 == 0):
+                    a_tp(pair, slot, me.lanes(step), step).wait_recv()
             a_tp(pair, 2, me.lanes(2), 1).wait_recv()
             start(a_sibling(pair, me.c))
         a_done[0] += count
@@ -486,32 +494,33 @@
     b_plane = gather_plane(
         me, b_block, start, (gb_send, gb_recv), lambda *at: start(b_sibling(*at, me.c))
     )
-    start(b_tp(0, me.lanes(0), 1))
-    start(b_tp(1, me.lanes(0), 3))
+    for slot, step in ((0, 1), (1, 3), (2, 2)):
+        start(b_tp(slot, me.lanes(0), step))
+    next(a_plane)
+    next(a_plane)
+    a_pass_on(1)
     next(a_plane)
     b_tp(0, me.lanes(3), 1).wait_recv()
     b_tp(1, me.lanes(1), 1).wait_recv()
-    start(b_tp(2, me.lanes(3 - 2 * me.c), 1 + 2 * me.c))
-    next(a_plane)
-    a_pass_on(1)
     b_tp(2, me.lanes(2), 1).wait_recv()
-    next(b_plane)
-    for _ in range(5):
-        next(a_plane)
     next(b_plane)
     for _ in range(4):
         next(a_plane)
+    a_pass_on(3)
+    for _ in range(4):
+        next(a_plane)
+    next(b_plane)
+    next(b_plane)
+    a_pass_on(PASSED - 4)
+    next(b_plane)
+    next(b_plane)
     for _ in range(2):
+        a_finish(3)
         next(b_plane)
-        a_pass_on(3)
-    for _ in range(3):
+    for _ in range(4):
+        a_finish(2)
         next(b_plane)
-        a_pass_on(3)
-        a_finish(3)
-    for _ in range(4):
-        next(b_plane)
-        a_finish(2)
-    a_finish(16 - a_done[0])
+    a_finish(16)
     for half in range(2):
         for j in range(4):
             for k in range(4):
@@ -554,111 +563,116 @@
             sib_here.add(pair)
             from_core(pair, me.c).wait_recv()
 
+    def ya_rows(pair):
+        return rows_of(me.at(*pair, me.c), 0, SUM_A)
+
     def ya_far(pair, step):
         n = pair[0] * 4 + pair[1]
         return remote(
-            contrib.at[rows_of(me.at(*pair, me.c), 0, PART_A), me.lanes(2)], ya_pass.at[n],
+            contrib.at[ya_rows(pair), me.lanes(2)], ya_pass.at[n],
             yp_send.at[n], yp_recv.at[n], me.tp_peer(step),
         )
 
     def ya_near(pair, step):
         n = pair[0] * 4 + pair[1]
-        slot = 0 if step == 1 else 1
-        return remote(
-            contrib.at[rows_of(me.at(*pair, me.c), 0, PART_A), me.lanes(step)], ya_ring.at[n, slot],
-            yr_send.at[n, slot], yr_recv.at[n, slot], me.tp_peer(step),
-        )
+        return remote(
+            contrib.at[ya_rows(pair), me.lanes(step)], ya_ring.at[n, step - 1],
+            yr_send.at[n, step - 1], yr_recv.at[n, step - 1], me.tp_peer(step),
+        )
+
+    passed_pairs = []
 
     def a_first(pair):
         sibling_here(pair)
-        at = rows_of(me.at(*pair, me.c), 0, PART_A)
-        theirs = from_sib[pair[0] * 4 + pair[1], :PART_A, :]
+        at = ya_rows(pair)
+        theirs = from_sib[pair[0] * 4 + pair[1], :SUM_A, :]
         contrib[at, :] = (contrib[at, :].astype(F32) + theirs.astype(F32)).astype(BF16)
-        far_step = 1 if sum(pair) % 2 == 0 else 3
-        start(ya_far(pair, far_step))
-        start(ya_near(pair, 4 - far_step))
+        if len(passed_pairs) < SUM_PASSED:
+            passed_pairs.append(pair)
+            far_step = 1 if sum(pair) % 2 == 0 else 3
+            start(ya_far(pair, far_step))
+            start(ya_near(pair, 4 - far_step))
+        else:
+            for step in (1, 3, 2):
+                start(ya_near(pair, step))
 
     def a_second(pair):
         step = 1 if sum(pair) % 2 == 0 else 3
         ya_far(pair, step).wait_recv()
-        at = rows_of(me.at(*pair, me.c), 0, PART_A)
+        at = ya_rows(pair)
         passed = ya_pass[pair[0] * 4 + pair[1]].astype(F32)
         contrib[at, me.lanes(step)] = (contrib[at, me.lanes(step)].astype(F32) + passed).astype(BF16)
         start(ya_near(pair, step))
 
     def a_third(pair):
         n = pair[0] * 4 + pair[1]
-        value = contrib[rows_of(me.at(*pair, me.c), 0, PART_A), own_lanes].astype(F32)
-        for step in (1, 3):
+        value = contrib[ya_rows(pair), own_lanes].astype(F32)
+        for step in (1, 3) if pair in passed_pairs else (1, 3, 2):
             ya_near(pair, step).wait_recv()
-            value = value + ya_ring[n, 0 if step == 1 else 1].astype(F32)
+            value = value + ya_ring[n, step - 1].astype(F32)
         a_sum[n] = value.astype(BF16)
 
     def a_own(half, j, k):
-        a = lax.rem(me.first(half) + j, 4)
-        b = lax.rem(me.second(half) + k, 4)
-        dz, dx = (k, j) if half == 0 else (j, k)
-        return a_sum.at[dz * 4 + dx, pl.ds(half * (PART_A // 2), PART_A // 2), :]
+        dz, dx = pair_of(half, j, k)
+        return a_sum.at[dz * 4 + dx, pl.ds(half * (SUM_A // 2), SUM_A // 2), :]
 
     def a_touch(half, j, k):
         return a_own(half, j, k)[...].astype(F32)
 
     def a_final(half, value):
-        at = pl.ds(half * (PART_A // 2), PART_A // 2)
+        at = pl.ds(half * (SUM_A // 2), SUM_A // 2)
         out[at, :] = (hid[at, :] + value).astype(BF16)
 
     def b_own(half, j, k):
         return contrib.at[
-            rows_of(me.block(half, j, k, me.c), PART_A + half * (PART_B // 2), PART_B // 2), :
+            rows_of(me.block(half, j, k, me.c), SUM_A + half * (SUM_B // 2), SUM_B // 2), :
         ]
 
     def b_touch(half, j, k):
         pair = pair_of(half, j, k)
         sibling_here(pair)
         theirs = from_sib[
-            pair[0] * 4 + pair[1], pl.ds(PART_A + half * (PART_B // 2), PART_B // 2), :
+            pair[0] * 4 + pair[1], pl.ds(SUM_A + half * (SUM_B // 2), SUM_B // 2), :
         ]
         return b_own(half, j, k)[...].astype(F32) + theirs.astype(F32)
 
     def b_final(half, value):
-        at = pl.ds(half * (PART_B // 2), PART_B // 2)
+        at = pl.ds(half * (SUM_B // 2), SUM_B // 2)
         plane_sum[at, :] = value
         plane_sum_b[at, :] = value.astype(BF16)
 
     a_back = scatter_plane(
         me, a_own, a_touch, a_final, start, (a_pass, a_ring, a_line),
-        (ap_send, ap_recv, ar_send, ar_recv, al_send, al_recv),
+        (ap_send, ap_recv, ar_send, ar_recv, al_send, al_recv), False,
     )
     b_back = scatter_plane(
         me, b_own, b_touch, b_final, start, (b_pass, b_ring, b_line),
-        (bp_send, bp_recv, br_send, br_recv, bl_send, bl_recv),
+        (bp_send, bp_recv, br_send, br_recv, bl_send, bl_recv), True,
     )
-    order = [(2, 2), (2, 0), (0, 2), (2, 1), (1, 2), (2, 3), (3, 2)]
-    order += [pair for pair in pairs if pair not in order]
+    order = [(2, 2), (2, 1), (1, 2), (3, 2), (2, 3), (1, 1), (1, 3), (3, 1), (3, 3)]
+    order += [(2, 0), (0, 2), (1, 0), (0, 1), (3, 0), (0, 3), (0, 0)]
     for n, pair in enumerate(order):
         compute(pair)
-        if n >= 8:
-            a_first(order[n - 8])
-    for n in range(4):
+        if n in (3, 6, 9, 12):
+            next(b_back)
+        if n >= 3:
+            a_first(order[n - 3])
+        if n >= 14:
+            a_second(order[n - 14])
+    for n in range(13, 16):
+        a_first(order[n])
+        a_second(order[n - 11])
+    next(b_back)
+    next(b_back)
+    for n in range(5, SUM_PASSED):
+        a_second(order[n])
+    for pair in order:
+        a_third(pair)
+    for _ in range(6):
+        next(a_back)
+    for _ in range(3):
         next(b_back)
-        a_first(order[8 + 2 * n])
-        a_first(order[9 + 2 * n])
-        a_second(order[2 * n])
-        a_second(order[2 * n + 1])
-    for n in range(4):
-        next(b_back)
-        a_second(order[8 + 2 * n])
-        a_second(order[9 + 2 * n])
-        a_third(order[2 * n])
-        a_third(order[2 * n + 1])
-    for _ in range(2):
-        next(b_back)
-    for _ in range(4):
-        next(a_back)
-    for n in range(8, 16):
-        a_third(order[n])
-    next(b_back)
-    for _ in range(4):
+    for _ in range(3):
         next(a_back)
     next(b_back)
 
@@ -670,13 +684,12 @@
 
     for step in (2, 1, 3):
         start(b_tp_sum(step))
-    for _ in range(4):
-        next(a_back)
+    next(a_back)
     moe = plane_sum[:, own_lanes]
-    for step in (1, 2, 3):
+    for step in (1, 3, 2):
         b_tp_sum(step).wait_recv()
         moe = moe + tp_r[step - 1].astype(F32)
-    out[PART_A:, :] = (hid[PART_A:, :] + moe).astype(BF16)
+    out[SUM_A:, :] = (hid[SUM_A:, :] + moe).astype(BF16)
 
     for copy in sent:
         copy.wait_send()
@@ -712,29 +725,29 @@
         pltpu.VMEM((UNITS, ROWS), BF16),
         pltpu.VMEM((D, ROWS), BF16),
         pltpu.VMEM((16, COLS, ROWS), BF16),
-        pltpu.VMEM((PART_B, ROWS), F32),
-        pltpu.VMEM((PART_B, ROWS), BF16),
-        pltpu.VMEM((3, PART_B, TP_ROWS), BF16),
+        pltpu.VMEM((SUM_B, ROWS), F32),
+        pltpu.VMEM((SUM_B, ROWS), BF16),
+        pltpu.VMEM((3, SUM_B, TP_ROWS), BF16),
         pltpu.VMEM((1, ROWS), F32),
-        pltpu.VMEM((2, 4, PART_B // 2, ROWS), BF16),
-        pltpu.VMEM((2, 8, PART_B // 2, ROWS), BF16),
-        pltpu.VMEM((2, 3, PART_B // 2, ROWS), BF16),
-        pltpu.VMEM((2, 4, PART_A // 2, TP_ROWS), BF16),
-        pltpu.VMEM((2, 8, PART_A // 2, TP_ROWS), BF16),
-        pltpu.VMEM((2, 3, PART_A // 2, TP_ROWS), BF16),
-        pltpu.VMEM((16, PART_A, TP_ROWS), BF16),
-        pltpu.VMEM((16, PART_A, TP_ROWS), BF16),
-        pltpu.VMEM((16, 2, PART_A, TP_ROWS), BF16),
+        pltpu.VMEM((2, 2, SUM_B // 2, ROWS), BF16),
+        pltpu.VMEM((2, 12, SUM_B // 2, ROWS), BF16),
+        pltpu.VMEM((2, 3, SUM_B // 2, ROWS), BF16),
+        pltpu.VMEM((2, 2, SUM_A // 2, TP_ROWS), BF16),
+        pltpu.VMEM((2, 12, SUM_A // 2, TP_ROWS), BF16),
+        pltpu.VMEM((2, 3, SUM_A // 2, TP_ROWS), BF16),
+        pltpu.VMEM((16, SUM_A, TP_ROWS), BF16),
+        pltpu.VMEM((16, SUM_A, TP_ROWS), BF16),
+        pltpu.VMEM((16, 3, SUM_A, TP_ROWS), BF16),
         dma((11,)),
         dma((4, 3)), dma((4, 3)),
-        dma((2, 15)), dma((2, 16)), dma((2, 16)), dma((2, 16)),
+        dma((2, 16)), dma((2, 16)), dma((2, 16)), dma((2, 16)),
         dma((3,)), dma((3,)),
         dma((3,)), dma((3,)),
-        dma((2, 15)), dma((2, 16)), dma((16, 3)), dma((16, 3)), dma((16,)), dma((16,)),
-        dma((2, 15)), dma((2, 16)), dma((2, 16)), dma((2, 16)),
-        dma((16,)), dma((16,)), dma((16,)), dma((16,)), dma((16, 2)), dma((16, 2)),
-        dma((2, 4)), dma((2, 4)), dma((2, 8)), dma((2, 8)), dma((2, 3)), dma((2, 3)),
-        dma((2, 4)), dma((2, 4)), dma((2, 8)), dma((2, 8)), dma((2, 3)), dma((2, 3)),
+        dma((2, 16)), dma((2, 16)), dma((16, 3)), dma((16, 3)), dma((16,)), dma((16,)),
+        dma((2, 16)), dma((2, 16)), dma((2, 16)), dma((2, 16)),
+        dma((16,)), dma((16,)), dma((16,)), dma((16,)), dma((16, 3)), dma((16, 3)),
+        dma((2, 2)), dma((2, 2)), dma((2, 12)), dma((2, 12)), dma((2, 3)), dma((2, 3)),
+        dma((2, 2)), dma((2, 2)), dma((2, 12)), dma((2, 12)), dma((2, 3)), dma((2, 3)),
         dma((3,)), dma((3,)),
     ]
     return pl.pallas_call(

time: 115 us -> 109 us (0.948)
  Pallas kernels: 113 us -> 108 us
    pallas_call x1, Pallas kernels: 113 us -> 108 us  [local(): pl.pallas_call(kernel, out_shape=jax.ShapeDtypeStruct((COLS, TP_ROWS), BF...]
where the time goes in v3:
time: 109 us
  Pallas kernels  108 us (99%)
  local copies, waits for them, and re-layouts  1.45 us (1%)
    pallas_call x1, Pallas kernels, local(): pl.pallas_call(kernel, out_shape=jax.ShapeDtypeStruct((COLS, TP_ROWS), BF...  108 us

profile of v3, /device:TPU:0, one launch (start us, length us, event | category | flops | bytes accessed | tf_op | source)
XLA Modules:
  0.0 109.3 jit_solution(15763690363316537661)
XLA Ops:
  0.0 107.8 %decode_step.1 = bf16[224,128]{1,0:T(8,128)(2,1)} custom-call(s32[4]{0:T(128)} %lengths.1, bf16[4,576,128]{2,1,0:T(8,128)(2,1)} %bitcast.16, bf16[4,576,1024]{2,1,0:T(8,128)(2,1)} %bitcast.11, bf16[32,512,128]{2,1,0:T(8,128)(2,1)} %uv_hbm.1, bf16[224,4096]{1,0:T(8,128)(2,1)} %bitcast.15, bf16[224,512]{1,0:T(8,128)(2,1)} %bitcast.17, f32[56,128]{1,0:T(8,128)} %bitcast.19, ...), custom_call_target="tpu_custom_call" | custom-call | tf_op jit(solution)/shard_map/decode_step/pallas_call | solution.py:753
  107.8 1.4 %copy.14 = bf16[128,224]{0,1:T(8,128)(2,1)} copy(bf16[128,224]{0,1:T(8,128)(2,1)} %bitcast.18) | data formatting | bytes 114688

commit v4 on v3

--- a/solution.py
+++ b/solution.py
@@ -16,6 +16,7 @@
 CTX = 1024
 HEADS = 128
 OWN_HEADS = 32
+HALF_HEADS = 16
 VHEAD = 128
 ROWS = 512
 OWN_ROWS = 4
@@ -32,10 +33,10 @@
 score_scale = 192.0 ** (-0.5)
 epsilon = 1e-06
 
-SUM_A = 64
-SUM_B = 160
-PASSED = 10
-SUM_PASSED = 8
+SUM_A = 96
+SUM_B = 128
+PASSED = 12
+SUM_PASSED = 12
 
 
 def tn_dot(a, b):
@@ -82,6 +83,9 @@
     def second_peer(self, half, step):
         return self.first_peer(1 - half, step)
 
+    def pair_peer(self, pair):
+        return (self.at(*pair, self.c), self.y)
+
     def lanes(self, step):
         at = lax.rem(self.y + step, 4) * TP_ROWS
         return pl.ds(pl.multiple_of(at, TP_ROWS), TP_ROWS)
@@ -129,17 +133,15 @@
     def second_axis(half, j):
         send(half, j, 0, me.second_peer(half, 1), j, 3)
         send(half, j, 0, me.second_peer(half, 3), j, 1)
-        if j > 1:
+        if j == 2:
             send(half, j, 0, me.second_peer(half, 2), j, 2)
 
     for half in range(2):
         for step in (1, 3, 2):
             send(half, 0, 0, me.first_peer(half, step), 4 - step, 0)
-    for half in range(2):
         second_axis(half, 0)
-    for half in range(2):
         landed(half, 0, 0)
-    yield
+        yield
     for j in (1, 3):
         for half in range(2):
             arrived(half, j, 0)
@@ -162,6 +164,8 @@
             arrived(half, j, 1)
             if j == 1:
                 send(half, j, 1, me.second_peer(half, 3), j, 2)
+            if j == 3:
+                send(half, j, 3 - 2 * me.c, me.second_peer(half, 1 + 2 * me.c), j, 2)
         for half in range(2):
             landed(half, j, 3)
             landed(half, j, 1)
@@ -173,7 +177,7 @@
         yield
 
 
-def scatter_plane(me, own, touch, finish, start, bufs, sems, passing):
+def scatter_plane(me, own, touch, finish, start, bufs, sems):
     pass_r, ring_r, line_r = bufs
     pass_send, pass_recv, ring_send, ring_recv, line_send, line_recv = sems
 
@@ -212,7 +216,7 @@
     def gathered(half, j):
         value = touch(half, j, 0)
         for k in (1, 3, 2):
-            if k == 2 and passing and j in (1, 2):
+            if k == 2 and j in (1, 2):
                 continue
             near(half, j, k).wait_recv()
             value = value + ring_r[half, j * 3 + k - 1].astype(F32)
@@ -221,7 +225,7 @@
     for j in (2, 1):
         for half in range(2):
             own(half, j, 2)[...] = touch(half, j, 2).astype(BF16)
-            start(far(half, j) if passing else near(half, j, 2))
+            start(far(half, j))
         yield
     give(2, 3)
     give(1, 1)
@@ -230,8 +234,8 @@
     give(3, 1)
     give(3, 3)
     yield
-    (give_passed if passing else give)(2, 1)
-    (give_passed if passing else give)(1, 3)
+    give_passed(2, 1)
+    give_passed(1, 3)
     yield
     give(0, 2)
     give(0, 1)
@@ -252,18 +256,18 @@
 
 
 def kernel(
-    lengths, q_hbm, cache_hbm, uv_hbm, out_w_hbm, residual_hbm, gain, gate_hbm, up_hbm, down_hbm,
-    routes, route_weights, out,
-    qv, cv, uv, out_w, res, down_w, gate_up_t, down_t,
+    lengths, q_hbm, cache_hbm, uv_hbm, out_w_hbm, residual_hbm, gain_hbm, gate_hbm, up_hbm, down_hbm,
+    routes_hbm, route_weights_hbm, out,
+    gain, routes, route_weights, qv, cv, uv, out_w, res, down_w, gate_up_t, down_t,
     ctx, by_head, by_head_f, heads_all, part, part_b, part_r, hid, hid_t, gate_up,
     act, contrib, from_sib, plane_sum, plane_sum_b, tp_r, weight_row,
-    b_pass, b_ring, b_line, a_pass, a_ring, a_line, a_sum, ya_pass, ya_ring,
+    b_pass, b_ring, b_line, a_ring, a_sum, ya_pass, ya_ring,
     load_sem, a2a_send, a2a_recv, ag_send, ag_recv, ag_sib_send, ag_sib_recv,
     rs_send, rs_recv, hy_send, hy_recv,
     ga_send, ga_recv, gy_send, gy_recv, ga_sib_send, ga_sib_recv,
     gb_send, gb_recv, gb_sib_send, gb_sib_recv,
     sib_send, sib_recv, yp_send, yp_recv, yr_send, yr_recv,
-    ap_send, ap_recv, ar_send, ar_recv, al_send, al_recv,
+    ar_send, ar_recv,
     bp_send, bp_recv, br_send, br_recv, bl_send, bl_recv,
     tp_send, tp_recv,
 ):
@@ -296,6 +300,15 @@
         peers += [me.first_peer(0, step), me.first_peer(1, step), me.tp_peer(step)]
     for peer in peers:
         pl.semaphore_signal(barrier, inc=1, device_id=peer, device_id_type=MESH)
+
+    def heads_out(row, half, step):
+        to = lax.rem(y + step, 4) * OWN_HEADS + half * HALF_HEADS
+        return remote(
+            ctx.at[row, pl.ds(pl.multiple_of(to, HALF_HEADS), HALF_HEADS)],
+            by_head.at[y * OWN_ROWS + row, pl.ds(half * HALF_HEADS, HALF_HEADS)],
+            a2a_send.at[row, half * 3 + step - 1], a2a_recv.at[row, half * 3 + step - 1],
+            me.tp_peer(step),
+        )
 
     ready("q")
     for i in range(OWN_ROWS):
@@ -308,6 +321,9 @@
             load("gate", gate_hbm, contrib.at[:, pl.ds(0, UNITS)], 8)
             load("up", up_hbm, contrib.at[:, pl.ds(UNITS, UNITS)], 9)
             load("down", down_hbm, down_w, 10)
+            load("gain", gain_hbm, gain, 11)
+            load("routes", routes_hbm, routes, 12)
+            load("route_weights", route_weights_hbm, route_weights, 13)
         scores = tn_dot(qv[i], cv[i]) * score_scale
         usable = lax.broadcasted_iota(jnp.int32, scores.shape, 1) < lengths[i]
         peak = jnp.max(jnp.where(usable, scores, -1e30), axis=1, keepdims=True)
@@ -315,48 +331,42 @@
         total = jnp.sum(soft, axis=1, keepdims=True)
         summed = nt_dot(soft.astype(BF16), cv[i, :LAT, :])
         ctx[i] = (summed / total).astype(BF16)
-        if i < 2:
-            continue
-        if i == 2:
+        if i == 0:
             pl.semaphore_wait(barrier, len(peers))
-        for row in range(3) if i == 2 else (3,):
-            for step in (2, 1, 3):
-                to = pl.multiple_of(lax.rem(y + step, 4) * OWN_HEADS, OWN_HEADS)
-                start(remote(
-                    ctx.at[row, pl.ds(to, OWN_HEADS)], by_head.at[y * OWN_ROWS + row],
-                    a2a_send.at[row, step - 1], a2a_recv.at[row, step - 1], me.tp_peer(step),
-                ))
-            by_head[y * OWN_ROWS + row] = ctx[
-                row, pl.ds(pl.multiple_of(y * OWN_HEADS, OWN_HEADS), OWN_HEADS), :
-            ]
+        for step in (2, 1, 3):
+            start(heads_out(i, 0, step))
+        by_head[y * OWN_ROWS + i] = ctx[
+            i, pl.ds(pl.multiple_of(y * OWN_HEADS, OWN_HEADS), OWN_HEADS), :
+        ]
     for i in range(OWN_ROWS):
-        for step in (1, 2, 3):
-            source = lax.rem(y + 4 - step, 4)
-            remote(
-                ctx.at[i, pl.ds(0, OWN_HEADS)],
-                by_head.at[source * OWN_ROWS + i],
-                a2a_send.at[i, step - 1],
-                a2a_recv.at[i, step - 1],
-                me.tp_peer(step),
-            ).wait_recv()
+        for step in (2, 1, 3):
+            start(heads_out(i, 1, step))
 
     ready("uv")
-    for part_of in range(LAT // 128):
-        piece = by_head[:, :, pl.ds(part_of * 128, 128)]
-        by_head_f[part_of] = piece.astype(F32).reshape(DP_ROWS * OWN_HEADS, 128)
     own_rows = pl.ds(pl.multiple_of(d * DP_ROWS, DP_ROWS), DP_ROWS)
-    for h in range(OWN_HEADS):
-        picked = jnp.concatenate(
-            [
-                by_head_f[part_of, pl.ds(h, DP_ROWS, stride=OWN_HEADS), :]
-                for part_of in range(LAT // 128)
-            ],
-            axis=1,
-        ).astype(BF16)
-        heads_all[own_rows, pl.ds(h * VHEAD, VHEAD)] = jnp.dot(
-            picked, uv[h], preferred_element_type=F32
-        ).astype(BF16)
-
+
+    def project(half):
+        for i in range(OWN_ROWS):
+            for step in (1, 3, 2):
+                heads_out(i, half, step).wait_recv()
+        heads = pl.ds(half * HALF_HEADS, HALF_HEADS)
+        for part_of in range(LAT // 128):
+            piece = by_head[:, heads, pl.ds(part_of * 128, 128)]
+            by_head_f[part_of] = piece.astype(F32).reshape(DP_ROWS * HALF_HEADS, 128)
+        for h in range(HALF_HEADS):
+            picked = jnp.concatenate(
+                [
+                    by_head_f[part_of, pl.ds(h, DP_ROWS, stride=HALF_HEADS), :]
+                    for part_of in range(LAT // 128)
+                ],
+                axis=1,
+            ).astype(BF16)
+            at = half * HALF_HEADS + h
+            heads_all[own_rows, pl.ds(at * VHEAD, VHEAD)] = jnp.dot(
+                picked, uv[at], preferred_element_type=F32
+            ).astype(BF16)
+
+    project(0)
     def head_block(half, dp):
         return heads_all.at[
             pl.ds(pl.multiple_of(dp * DP_ROWS, DP_ROWS), DP_ROWS), pl.ds(half * (INNER // 2), INNER // 2)
@@ -376,30 +386,32 @@
         return carry
 
     turned_to = 0
-    for step in gather_plane(
+    heads_plane = gather_plane(
         me, head_block, start, (ag_send, ag_recv), lambda *at: start(head_sibling(*at, me.c))
-    ):
+    )
+    next(heads_plane)
+    project(1)
+    for step in heads_plane:
         if turned_to == 0:
-            ready("gate")
-            ready("up")
-            ready("down")
+            for name in ("gate", "up", "down", "gain"):
+                ready(name)
         upto = min(turned_to + 7, D // 128)
         lax.fori_loop(turned_to, upto, turn_step, 0)
         turned_to = upto
+
+    ready("out_w")
+    part[...] = jnp.zeros_like(part)
+
+    def out_step(k, carry):
+        at = pl.ds(pl.multiple_of(k * 512, 512), 512)
+        part[...] += nt_dot(out_w[:, at], heads_all[:, at])
+        return carry
+
     for half in range(2):
         for j in range(4):
             for k in range(4):
                 head_sibling(half, j, k, 1 - me.c).wait_recv()
-
-    ready("out_w")
-    part[...] = jnp.zeros_like(part)
-
-    def out_step(k, carry):
-        at = pl.ds(pl.multiple_of(k * 512, 512), 512)
-        part[...] += nt_dot(out_w[:, at], heads_all[:, at])
-        return carry
-
-    lax.fori_loop(0, INNER // 512, out_step, 0)
+        lax.fori_loop(half * 4, half * 4 + 4, out_step, 0)
     for block in range(4):
         part_b[block] = part[:, block * TP_ROWS : (block + 1) * TP_ROWS].astype(BF16)
     for step in (2, 1, 3):
@@ -408,6 +420,8 @@
             rs_send.at[step - 1], rs_recv.at[step - 1], me.tp_peer(step),
         ))
 
+    ready("routes")
+    ready("route_weights")
     weight_row[...] = jnp.sum(
         jnp.where(routes[...] == d, route_weights[...], 0.0), axis=0, keepdims=True
     )
@@ -427,9 +441,6 @@
 
     pairs = [(dz, dx) for dz in range(4) for dx in range(4)]
 
-    def a_block(half, dp):
-        return hid_t.at[rows_of(dp, half * (PART_A // 2), PART_A // 2), own_lanes]
-
     def b_block(half, dp):
         return hid_t.at[rows_of(dp, PART_A + half * (PART_B // 2), PART_B // 2), :]
 
@@ -446,17 +457,19 @@
         n = pair[0] * 4 + pair[1]
         return remote(ref, ref, ga_sib_send.at[n], ga_sib_recv.at[n], me.sibling())
 
-    a_halves, a_landed = set(), []
-
-    def a_here(half, j, k):
-        pair = pair_of(half, j, k)
-        if pair in a_halves:
-            a_landed.append(pair)
-            start(a_tp(pair, 0, me.lanes(0), 1))
-            start(a_tp(pair, 1, me.lanes(0), 3))
-            if len(a_landed) > PASSED:
-                start(a_tp(pair, 2, me.lanes(0), 2))
-        a_halves.add(pair)
+    def a_plane(pair):
+        ref = hid_t.at[rows_of(d, 0, PART_A), own_lanes]
+        n, opposite = pair[0] * 4 + pair[1], (4 - pair[0]) % 4 * 4 + (4 - pair[1]) % 4
+        return remote(ref, ref, ga_send.at[n], ga_recv.at[opposite], me.pair_peer(pair))
+
+    a_landed = []
+
+    def a_here(pair):
+        a_landed.append(pair)
+        start(a_tp(pair, 0, me.lanes(0), 1))
+        start(a_tp(pair, 1, me.lanes(0), 3))
+        if len(a_landed) > PASSED:
+            start(a_tp(pair, 2, me.lanes(0), 2))
 
     a_passed, a_done = [0], [0]
 
@@ -490,30 +503,37 @@
         ref = hid_t.at[rows_of(d, PART_A, PART_B), lanes]
         return remote(ref, ref, hy_send.at[slot], hy_recv.at[slot], me.tp_peer(step))
 
-    a_plane = gather_plane(me, a_block, start, (ga_send, ga_recv), a_here)
     b_plane = gather_plane(
         me, b_block, start, (gb_send, gb_recv), lambda *at: start(b_sibling(*at, me.c))
     )
+    nearest = sorted(pairs, key=lambda pair: sum((0, 1, 2, 1)[step] for step in pair))
     for slot, step in ((0, 1), (1, 3), (2, 2)):
         start(b_tp(slot, me.lanes(0), step))
-    next(a_plane)
-    next(a_plane)
-    a_pass_on(1)
-    next(a_plane)
+    for pair in nearest[1:]:
+        start(a_plane(pair))
+    a_here((0, 0))
+    for pair in nearest[1:5]:
+        opposite = ((4 - pair[0]) % 4, (4 - pair[1]) % 4)
+        a_plane(opposite).wait_recv()
+        a_here(pair)
     b_tp(0, me.lanes(3), 1).wait_recv()
     b_tp(1, me.lanes(1), 1).wait_recv()
     b_tp(2, me.lanes(2), 1).wait_recv()
     next(b_plane)
-    for _ in range(4):
-        next(a_plane)
+    next(b_plane)
+    a_pass_on(1)
+    for pair in nearest[5:]:
+        opposite = ((4 - pair[0]) % 4, (4 - pair[1]) % 4)
+        a_plane(opposite).wait_recv()
+        a_here(pair)
     a_pass_on(3)
-    for _ in range(4):
-        next(a_plane)
     next(b_plane)
     next(b_plane)
-    a_pass_on(PASSED - 4)
+    a_pass_on(4)
     next(b_plane)
+    a_pass_on(2)
     next(b_plane)
+    a_pass_on(2)
     for _ in range(2):
         a_finish(3)
         next(b_plane)
@@ -604,6 +624,12 @@
         contrib[at, me.lanes(step)] = (contrib[at, me.lanes(step)].astype(F32) + passed).astype(BF16)
         start(ya_near(pair, step))
 
+    def a_give(pair):
+        n = pair[0] * 4 + pair[1]
+        return remote(
+            a_sum.at[n], a_ring.at[n - 1], ar_send.at[n - 1], ar_recv.at[n - 1], me.pair_peer(pair)
+        )
+
     def a_third(pair):
         n = pair[0] * 4 + pair[1]
         value = contrib[ya_rows(pair), own_lanes].astype(F32)
@@ -611,17 +637,8 @@
             ya_near(pair, step).wait_recv()
             value = value + ya_ring[n, step - 1].astype(F32)
         a_sum[n] = value.astype(BF16)
-
-    def a_own(half, j, k):
-        dz, dx = pair_of(half, j, k)
-        return a_sum.at[dz * 4 + dx, pl.ds(half * (SUM_A // 2), SUM_A // 2), :]
-
-    def a_touch(half, j, k):
-        return a_own(half, j, k)[...].astype(F32)
-
-    def a_final(half, value):
-        at = pl.ds(half * (SUM_A // 2), SUM_A // 2)
-        out[at, :] = (hid[at, :] + value).astype(BF16)
+        if n:
+            start(a_give(pair))
 
     def b_own(half, j, k):
         return contrib.at[
@@ -641,13 +658,9 @@
         plane_sum[at, :] = value
         plane_sum_b[at, :] = value.astype(BF16)
 
-    a_back = scatter_plane(
-        me, a_own, a_touch, a_final, start, (a_pass, a_ring, a_line),
-        (ap_send, ap_recv, ar_send, ar_recv, al_send, al_recv), False,
-    )
     b_back = scatter_plane(
         me, b_own, b_touch, b_final, start, (b_pass, b_ring, b_line),
-        (bp_send, bp_recv, br_send, br_recv, bl_send, bl_recv), True,
+        (bp_send, bp_recv, br_send, br_recv, bl_send, bl_recv),
     )
     order = [(2, 2), (2, 1), (1, 2), (3, 2), (2, 3), (1, 1), (1, 3), (3, 1), (3, 3)]
     order += [(2, 0), (0, 2), (1, 0), (0, 1), (3, 0), (0, 3), (0, 0)]
@@ -666,14 +679,12 @@
     next(b_back)
     for n in range(5, SUM_PASSED):
         a_second(order[n])
-    for pair in order:
+    for pair in order[:8]:
         a_third(pair)
-    for _ in range(6):
-        next(a_back)
     for _ in range(3):
         next(b_back)
-    for _ in range(3):
-        next(a_back)
+    for pair in order[8:]:
+        a_third(pair)
     next(b_back)
 
     def b_tp_sum(step):
@@ -684,7 +695,11 @@
 
     for step in (2, 1, 3):
         start(b_tp_sum(step))
-    next(a_back)
+    moe = a_sum[0].astype(F32)
+    for pair in order[:-1]:
+        a_give(pair).wait_recv()
+        moe = moe + a_ring[pair[0] * 4 + pair[1] - 1].astype(F32)
+    out[:SUM_A, :] = (hid[:SUM_A, :] + moe).astype(BF16)
     moe = plane_sum[:, own_lanes]
     for step in (1, 3, 2):
         b_tp_sum(step).wait_recv()
@@ -704,6 +719,9 @@
     smem = pl.BlockSpec(memory_space=pltpu.SMEM)
     dma = pltpu.SemaphoreType.DMA
     scratch = [
+        pltpu.VMEM((D // 128, 128), F32),
+        pltpu.VMEM(routes.shape[::-1], jnp.int32),
+        pltpu.VMEM(routes.shape[::-1], F32),
         pltpu.VMEM((OWN_ROWS, KEY, HEADS), BF16),
         pltpu.VMEM((OWN_ROWS, KEY, CTX), BF16),
         pltpu.VMEM((OWN_HEADS, LAT, VHEAD), BF16),
@@ -714,7 +732,7 @@
         pltpu.VMEM((D, UNITS), BF16),
         pltpu.VMEM((OWN_ROWS, HEADS, LAT), BF16),
         pltpu.VMEM((DP_ROWS, OWN_HEADS, LAT), BF16),
-        pltpu.VMEM((LAT // 128, DP_ROWS * OWN_HEADS, 128), F32),
+        pltpu.VMEM((LAT // 128, DP_ROWS * HALF_HEADS, 128), F32),
         pltpu.VMEM((ROWS, INNER), BF16),
         pltpu.VMEM((COLS, ROWS), F32),
         pltpu.VMEM((4, COLS, TP_ROWS), BF16),
@@ -732,28 +750,26 @@
         pltpu.VMEM((2, 2, SUM_B // 2, ROWS), BF16),
         pltpu.VMEM((2, 12, SUM_B // 2, ROWS), BF16),
         pltpu.VMEM((2, 3, SUM_B // 2, ROWS), BF16),
-        pltpu.VMEM((2, 2, SUM_A // 2, TP_ROWS), BF16),
-        pltpu.VMEM((2, 12, SUM_A // 2, TP_ROWS), BF16),
-        pltpu.VMEM((2, 3, SUM_A // 2, TP_ROWS), BF16),
+        pltpu.VMEM((15, SUM_A, TP_ROWS), BF16),
         pltpu.VMEM((16, SUM_A, TP_ROWS), BF16),
         pltpu.VMEM((16, SUM_A, TP_ROWS), BF16),
         pltpu.VMEM((16, 3, SUM_A, TP_ROWS), BF16),
-        dma((11,)),
-        dma((4, 3)), dma((4, 3)),
+        dma((14,)),
+        dma((4, 6)), dma((4, 6)),
         dma((2, 16)), dma((2, 16)), dma((2, 16)), dma((2, 16)),
         dma((3,)), dma((3,)),
         dma((3,)), dma((3,)),
-        dma((2, 16)), dma((2, 16)), dma((16, 3)), dma((16, 3)), dma((16,)), dma((16,)),
+        dma((16,)), dma((16,)), dma((16, 3)), dma((16, 3)), dma((16,)), dma((16,)),
         dma((2, 16)), dma((2, 16)), dma((2, 16)), dma((2, 16)),
         dma((16,)), dma((16,)), dma((16,)), dma((16,)), dma((16, 3)), dma((16, 3)),
-        dma((2, 2)), dma((2, 2)), dma((2, 12)), dma((2, 12)), dma((2, 3)), dma((2, 3)),
+        dma((15,)), dma((15,)),
         dma((2, 2)), dma((2, 2)), dma((2, 12)), dma((2, 12)), dma((2, 3)), dma((2, 3)),
         dma((3,)), dma((3,)),
     ]
     return pl.pallas_call(
         kernel,
         out_shape=jax.ShapeDtypeStruct((COLS, TP_ROWS), BF16),
-        in_specs=[smem] + [anywhere] * 5 + [vmem] + [anywhere] * 3 + [vmem] * 2,
+        in_specs=[smem] + [anywhere] * 11,
         out_specs=vmem,
         scratch_shapes=scratch,
         compiler_params=pltpu.CompilerParams(

time: 109 us -> 105 us (0.963)
  Pallas kernels: 108 us -> 103 us
    pallas_call x1, Pallas kernels: 108 us -> 103 us  [local(): pl.pallas_call(kernel, out_shape=jax.ShapeDtypeStruct((COLS, TP_ROWS), BF...]
where the time goes in v4:
time: 105 us
  Pallas kernels  103 us (98%)
  local copies, waits for them, and re-layouts  1.45 us (1%)
    pallas_call x1, Pallas kernels, local(): pl.pallas_call(kernel, out_shape=jax.ShapeDtypeStruct((COLS, TP_ROWS), BF...  103 us

profile of v4, /device:TPU:0, one launch (start us, length us, event | category | flops | bytes accessed | tf_op | source)
XLA Modules:
  0.0 104.5 jit_solution(3889017242080163553)
XLA Ops:
  0.0 103.1 %decode_step.1 = bf16[224,128]{1,0:T(8,128)(2,1)} custom-call(s32[4]{0:T(128)} %lengths.1, bf16[4,576,128]{2,1,0:T(8,128)(2,1)} %bitcast.16, bf16[4,576,1024]{2,1,0:T(8,128)(2,1)} %bitcast.11, bf16[32,512,128]{2,1,0:T(8,128)(2,1)} %uv_hbm.1, bf16[224,4096]{1,0:T(8,128)(2,1)} %bitcast.15, bf16[224,512]{1,0:T(8,128)(2,1)} %bitcast.17, f32[56,128]{1,0:T(8,128)} %bitcast.19, ...), custom_call_target="tpu_custom_call" | custom-call | tf_op jit(solution)/shard_map/decode_step/pallas_call | solution.py:769
  103.1 1.4 %copy.14 = bf16[128,224]{0,1:T(8,128)(2,1)} copy(bf16[128,224]{0,1:T(8,128)(2,1)} %bitcast.18) | data formatting | bytes 114688

commit v5 on v4

--- a/solution.py
+++ b/solution.py
@@ -1,4 +1,4 @@
-import functools
+import math
 
 import jax
 import jax.numpy as jnp
@@ -100,10 +100,32 @@
         return (z * 4 + x) * 2 + c
 
 
+class Sends:
+    def __init__(self, sems, group):
+        self.sem, self.total, self.at = sems.at[group], 0, self
+
+    def __getitem__(self, index):
+        return self
+
+
+class Copy:
+    def __init__(self, src, dst, send, recv, device):
+        self.sends, self.bytes = send, 2 * math.prod(src.shape)
+        self.copy = pltpu.make_async_remote_copy(
+            src_ref=src, dst_ref=dst, send_sem=send.sem, recv_sem=recv,
+            device_id=device, device_id_type=MESH,
+        )
+
+    def start(self):
+        self.sends.total += self.bytes
+        self.copy.start()
+
+    def wait_recv(self):
+        self.copy.wait_recv()
+
+
 def remote(src, dst, send, recv, device):
-    return pltpu.make_async_remote_copy(
-        src_ref=src, dst_ref=dst, send_sem=send, recv_sem=recv, device_id=device, device_id_type=MESH
-    )
+    return Copy(src, dst, send, recv, device)
 
 
 def rows_of(dp, offset, count):
@@ -112,7 +134,6 @@
 
 def gather_plane(me, blk, start, sems, landed):
     send_sem, recv_sem = sems
-    count = [0, 0]
 
     def ref_of(half, j, k):
         return blk(half, me.block(half, j, k, me.c))
@@ -120,14 +141,13 @@
     def send(half, j, k, device, rj, rk):
         ref = ref_of(half, j, k)
         start(remote(
-            ref, ref, send_sem.at[half, count[half]], recv_sem.at[half, rj * 4 + rk], device
+            ref, ref, send_sem, recv_sem.at[half, rj * 4 + rk], device
         ))
-        count[half] += 1
 
     def arrived(half, j, k):
         ref = ref_of(half, j, k)
         remote(
-            ref, ref, send_sem.at[half, 0], recv_sem.at[half, j * 4 + k], me.sibling()
+            ref, ref, send_sem, recv_sem.at[half, j * 4 + k], me.sibling()
         ).wait_recv()
 
     def second_axis(half, j):
@@ -177,27 +197,27 @@
         yield
 
 
-def scatter_plane(me, own, touch, finish, start, bufs, sems):
+def scatter_plane(me, own, touch, finish, start, all_here, bufs, sems):
     pass_r, ring_r, line_r = bufs
-    pass_send, pass_recv, ring_send, ring_recv, line_send, line_recv = sems
+    sends, pass_recv, ring_recv, line_recv = sems
 
     def far(half, j):
         return remote(
-            own(half, j, 2), pass_r.at[half, j - 1], pass_send.at[half, j - 1],
-            pass_recv.at[half, j - 1], me.second_peer(half, 1 if j == 2 else 3),
+            own(half, j, 2), pass_r.at[half, j - 1], sends, pass_recv.at[half, j - 1],
+            me.second_peer(half, 1 if j == 2 else 3),
         )
 
     def near(half, j, k):
         slot = j * 3 + k - 1
         return remote(
-            own(half, j, k), ring_r.at[half, slot], ring_send.at[half, slot],
-            ring_recv.at[half, slot], me.second_peer(half, k),
+            own(half, j, k), ring_r.at[half, slot], sends, ring_recv.at[half, j],
+            me.second_peer(half, k),
         )
 
     def line(half, j):
         return remote(
-            own(half, j, 0), line_r.at[half, j - 1], line_send.at[half, j - 1],
-            line_recv.at[half, j - 1], me.first_peer(half, j),
+            own(half, j, 0), line_r.at[half, j - 1], sends, line_recv.at[half],
+            me.first_peer(half, j),
         )
 
     def give(j, k):
@@ -215,10 +235,9 @@
 
     def gathered(half, j):
         value = touch(half, j, 0)
-        for k in (1, 3, 2):
-            if k == 2 and j in (1, 2):
-                continue
-            near(half, j, k).wait_recv()
+        steps = (1, 3) if j in (1, 2) else (1, 3, 2)
+        all_here(ring_r.at[half, pl.ds(0, len(steps))], ring_recv.at[half, j])
+        for k in steps:
             value = value + ring_r[half, j * 3 + k - 1].astype(F32)
         return value
 
@@ -248,8 +267,8 @@
         yield
     for half in range(2):
         value = gathered(half, 0)
+        all_here(line_r.at[half], line_recv.at[half])
         for j in (1, 3, 2):
-            line(half, j).wait_recv()
             value = value + line_r[half, j - 1].astype(F32)
         finish(half, value)
     yield
@@ -262,21 +281,17 @@
     ctx, by_head, by_head_f, heads_all, part, part_b, part_r, hid, hid_t, gate_up,
     act, contrib, from_sib, plane_sum, plane_sum_b, tp_r, weight_row,
     b_pass, b_ring, b_line, a_ring, a_sum, ya_pass, ya_ring,
-    load_sem, a2a_send, a2a_recv, ag_send, ag_recv, ag_sib_send, ag_sib_recv,
-    rs_send, rs_recv, hy_send, hy_recv,
-    ga_send, ga_recv, gy_send, gy_recv, ga_sib_send, ga_sib_recv,
-    gb_send, gb_recv, gb_sib_send, gb_sib_recv,
-    sib_send, sib_recv, yp_send, yp_recv, yr_send, yr_recv,
-    ar_send, ar_recv,
-    bp_send, bp_recv, br_send, br_recv, bl_send, bl_recv,
-    tp_send, tp_recv,
+    load_sem, send_sems, a2a_recv, ag_recv, ag_sib_recv, rs_recv, hy_recv,
+    ga_recv, gy_recv, gb_recv, gather_sib_recv,
+    sib_recv, yp_recv, yr_recv, ar_recv, bp_recv, br_recv, bl_recv, tp_recv,
 ):
     me = Place()
     y, d = me.y, me.d
     own_lanes = pl.ds(pl.multiple_of(y * TP_ROWS, TP_ROWS), TP_ROWS)
 
     loads = {}
-    sent = []
+    sends = [Sends(send_sems, group) for group in range(6)]
+    early_send, rs_send, gather_send, ga_send, sum_send, ar_send = sends
 
     def load(name, src, dst, index):
         copy = pltpu.make_async_copy(src, dst, load_sem.at[index])
@@ -288,7 +303,9 @@
 
     def start(copy):
         copy.start()
-        sent.append(copy)
+
+    def all_here(ref, recv):
+        remote(ref, ref, early_send, recv, me.sibling()).wait_recv()
 
     load("q", q_hbm, qv, 0)
     for i in range(OWN_ROWS):
@@ -306,8 +323,7 @@
         return remote(
             ctx.at[row, pl.ds(pl.multiple_of(to, HALF_HEADS), HALF_HEADS)],
             by_head.at[y * OWN_ROWS + row, pl.ds(half * HALF_HEADS, HALF_HEADS)],
-            a2a_send.at[row, half * 3 + step - 1], a2a_recv.at[row, half * 3 + step - 1],
-            me.tp_peer(step),
+            early_send, a2a_recv.at[half], me.tp_peer(step),
         )
 
     ready("q")
@@ -331,13 +347,15 @@
         total = jnp.sum(soft, axis=1, keepdims=True)
         summed = nt_dot(soft.astype(BF16), cv[i, :LAT, :])
         ctx[i] = (summed / total).astype(BF16)
-        if i == 0:
-            pl.semaphore_wait(barrier, len(peers))
-        for step in (2, 1, 3):
-            start(heads_out(i, 0, step))
         by_head[y * OWN_ROWS + i] = ctx[
             i, pl.ds(pl.multiple_of(y * OWN_HEADS, OWN_HEADS), OWN_HEADS), :
         ]
+        if i == 2:
+            pl.semaphore_wait(barrier, len(peers))
+        if i >= 2:
+            for row in (0, 1, 2) if i == 2 else (3,):
+                for step in (2, 1, 3):
+                    start(heads_out(row, 0, step))
     for i in range(OWN_ROWS):
         for step in (2, 1, 3):
             start(heads_out(i, 1, step))
@@ -346,9 +364,8 @@
     own_rows = pl.ds(pl.multiple_of(d * DP_ROWS, DP_ROWS), DP_ROWS)
 
     def project(half):
-        for i in range(OWN_ROWS):
-            for step in (1, 3, 2):
-                heads_out(i, half, step).wait_recv()
+        others = by_head.at[pl.ds(0, DP_ROWS - OWN_ROWS), pl.ds(0, HALF_HEADS)]
+        all_here(others, a2a_recv.at[half])
         heads = pl.ds(half * HALF_HEADS, HALF_HEADS)
         for part_of in range(LAT // 128):
             piece = by_head[:, heads, pl.ds(part_of * 128, 128)]
@@ -375,7 +392,7 @@
     def head_sibling(half, j, k, c):
         ref = head_block(half, me.block(half, j, k, c))
         return remote(
-            ref, ref, ag_sib_send.at[half, j * 4 + k], ag_sib_recv.at[half, j * 4 + k], me.sibling()
+            ref, ref, early_send, ag_sib_recv.at[half], me.sibling()
         )
 
     def turn_step(i, carry):
@@ -387,7 +404,7 @@
 
     turned_to = 0
     heads_plane = gather_plane(
-        me, head_block, start, (ag_send, ag_recv), lambda *at: start(head_sibling(*at, me.c))
+        me, head_block, start, (early_send, ag_recv), lambda *at: start(head_sibling(*at, me.c))
     )
     next(heads_plane)
     project(1)
@@ -408,16 +425,14 @@
         return carry
 
     for half in range(2):
-        for j in range(4):
-            for k in range(4):
-                head_sibling(half, j, k, 1 - me.c).wait_recv()
+        all_here(heads_all.at[pl.ds(0, ROWS // 2), pl.ds(0, INNER // 2)], ag_sib_recv.at[half])
         lax.fori_loop(half * 4, half * 4 + 4, out_step, 0)
     for block in range(4):
         part_b[block] = part[:, block * TP_ROWS : (block + 1) * TP_ROWS].astype(BF16)
     for step in (2, 1, 3):
         start(remote(
             part_b.at[lax.rem(y + step, 4)], part_r.at[step - 1],
-            rs_send.at[step - 1], rs_recv.at[step - 1], me.tp_peer(step),
+            rs_send, rs_recv.at[0], me.tp_peer(step),
         ))
 
     ready("routes")
@@ -428,11 +443,8 @@
 
     ready("res")
     total = res[...].astype(F32) + part[:, own_lanes]
+    all_here(part_r, rs_recv.at[0])
     for step in (1, 2, 3):
-        remote(
-            part_b.at[0], part_r.at[step - 1], rs_send.at[step - 1], rs_recv.at[step - 1],
-            me.tp_peer(step),
-        ).wait_recv()
         total = total + part_r[step - 1].astype(F32)
     hidden = total.astype(BF16)
     hid[...] = hidden.astype(F32)
@@ -447,20 +459,25 @@
     def pair_of(half, j, k):
         return (k, j) if half == 0 else (j, k)
 
+    nearest = sorted(pairs, key=lambda pair: sum((0, 1, 2, 1)[step] for step in pair))
+    passed_on = nearest[:PASSED]
+
     def a_tp(pair, slot, lanes, step):
         ref = hid_t.at[rows_of(me.at(*pair, me.c), 0, PART_A), lanes]
         n = pair[0] * 4 + pair[1]
-        return remote(ref, ref, gy_send.at[n, slot], gy_recv.at[n, slot], me.tp_peer(step))
+        alone = pair in passed_on and slot == sum(pair) % 2
+        return remote(
+            ref, ref, gather_send, gy_recv.at[n, 0 if alone else 1], me.tp_peer(step)
+        )
 
     def a_sibling(pair, c):
         ref = hid_t.at[rows_of(me.at(*pair, c), 0, PART_A), :]
-        n = pair[0] * 4 + pair[1]
-        return remote(ref, ref, ga_sib_send.at[n], ga_sib_recv.at[n], me.sibling())
+        return remote(ref, ref, gather_send, gather_sib_recv.at[0], me.sibling())
 
     def a_plane(pair):
         ref = hid_t.at[rows_of(d, 0, PART_A), own_lanes]
-        n, opposite = pair[0] * 4 + pair[1], (4 - pair[0]) % 4 * 4 + (4 - pair[1]) % 4
-        return remote(ref, ref, ga_send.at[n], ga_recv.at[opposite], me.pair_peer(pair))
+        opposite = (4 - pair[0]) % 4 * 4 + (4 - pair[1]) % 4
+        return remote(ref, ref, ga_send, ga_recv.at[opposite], me.pair_peer(pair))
 
     a_landed = []
 
@@ -486,29 +503,24 @@
     def a_finish(count):
         for n in range(a_done[0], min(a_done[0] + count, 16)):
             pair = a_landed[n]
-            for slot, step in ((1, 1), (0, 3)):
-                if n >= PASSED or (step == 1) == (sum(pair) % 2 == 0):
-                    a_tp(pair, slot, me.lanes(step), step).wait_recv()
-            a_tp(pair, 2, me.lanes(2), 1).wait_recv()
+            copies = 2 if pair in passed_on else 3
+            all_here(ya_pass.at[pl.ds(0, copies)], gy_recv.at[pair[0] * 4 + pair[1], 1])
             start(a_sibling(pair, me.c))
         a_done[0] += count
 
     def b_sibling(half, j, k, c):
         ref = b_block(half, me.block(half, j, k, c))
-        return remote(
-            ref, ref, gb_sib_send.at[half, j * 4 + k], gb_sib_recv.at[half, j * 4 + k], me.sibling()
-        )
-
-    def b_tp(slot, lanes, step):
+        return remote(ref, ref, gather_send, gather_sib_recv.at[0], me.sibling())
+
+    def b_tp(lanes, step):
         ref = hid_t.at[rows_of(d, PART_A, PART_B), lanes]
-        return remote(ref, ref, hy_send.at[slot], hy_recv.at[slot], me.tp_peer(step))
+        return remote(ref, ref, gather_send, hy_recv.at[0], me.tp_peer(step))
 
     b_plane = gather_plane(
-        me, b_block, start, (gb_send, gb_recv), lambda *at: start(b_sibling(*at, me.c))
+        me, b_block, start, (gather_send, gb_recv), lambda *at: start(b_sibling(*at, me.c))
     )
-    nearest = sorted(pairs, key=lambda pair: sum((0, 1, 2, 1)[step] for step in pair))
-    for slot, step in ((0, 1), (1, 3), (2, 2)):
-        start(b_tp(slot, me.lanes(0), step))
+    for step in (1, 3, 2):
+        start(b_tp(me.lanes(0), step))
     for pair in nearest[1:]:
         start(a_plane(pair))
     a_here((0, 0))
@@ -516,9 +528,7 @@
         opposite = ((4 - pair[0]) % 4, (4 - pair[1]) % 4)
         a_plane(opposite).wait_recv()
         a_here(pair)
-    b_tp(0, me.lanes(3), 1).wait_recv()
-    b_tp(1, me.lanes(1), 1).wait_recv()
-    b_tp(2, me.lanes(2), 1).wait_recv()
+    all_here(tp_r, hy_recv.at[0])
     next(b_plane)
     next(b_plane)
     a_pass_on(1)
@@ -541,12 +551,7 @@
         a_finish(2)
         next(b_plane)
     a_finish(16)
-    for half in range(2):
-        for j in range(4):
-            for k in range(4):
-                b_sibling(half, j, k, 1 - me.c).wait_recv()
-    for pair in pairs:
-        a_sibling(pair, 1 - me.c).wait_recv()
+    all_here(hid_t.at[pl.ds(0, D // 2)], gather_sib_recv.at[0])
 
     gate_up[...] = jnp.zeros_like(gate_up)
 
@@ -568,7 +573,7 @@
         n = pair[0] * 4 + pair[1]
         return remote(
             contrib.at[rows_of(me.at(*pair, c), 0, COLS), :], from_sib.at[n],
-            sib_send.at[n], sib_recv.at[n], me.sibling(),
+            sum_send, sib_recv.at[n], me.sibling(),
         )
 
     def compute(pair):
@@ -590,14 +595,14 @@
         n = pair[0] * 4 + pair[1]
         return remote(
             contrib.at[ya_rows(pair), me.lanes(2)], ya_pass.at[n],
-            yp_send.at[n], yp_recv.at[n], me.tp_peer(step),
+            sum_send, yp_recv.at[n], me.tp_peer(step),
         )
 
     def ya_near(pair, step):
         n = pair[0] * 4 + pair[1]
         return remote(
             contrib.at[ya_rows(pair), me.lanes(step)], ya_ring.at[n, step - 1],
-            yr_send.at[n, step - 1], yr_recv.at[n, step - 1], me.tp_peer(step),
+            sum_send, yr_recv.at[n], me.tp_peer(step),
         )
 
     passed_pairs = []
@@ -627,14 +632,15 @@
     def a_give(pair):
         n = pair[0] * 4 + pair[1]
         return remote(
-            a_sum.at[n], a_ring.at[n - 1], ar_send.at[n - 1], ar_recv.at[n - 1], me.pair_peer(pair)
+            a_sum.at[n], a_ring.at[n - 1], ar_send, ar_recv.at[0], me.pair_peer(pair)
         )
 
     def a_third(pair):
         n = pair[0] * 4 + pair[1]
         value = contrib[ya_rows(pair), own_lanes].astype(F32)
-        for step in (1, 3) if pair in passed_pairs else (1, 3, 2):
-            ya_near(pair, step).wait_recv()
+        steps = (1, 3) if pair in passed_pairs else (1, 3, 2)
+        all_here(ya_ring.at[n, pl.ds(0, len(steps))], yr_recv.at[n])
+        for step in steps:
             value = value + ya_ring[n, step - 1].astype(F32)
         a_sum[n] = value.astype(BF16)
         if n:
@@ -659,8 +665,8 @@
         plane_sum_b[at, :] = value.astype(BF16)
 
     b_back = scatter_plane(
-        me, b_own, b_touch, b_final, start, (b_pass, b_ring, b_line),
-        (bp_send, bp_recv, br_send, br_recv, bl_send, bl_recv),
+        me, b_own, b_touch, b_final, start, all_here, (b_pass, b_ring, b_line),
+        (sum_send, bp_recv, br_recv, bl_recv),
     )
     order = [(2, 2), (2, 1), (1, 2), (3, 2), (2, 3), (1, 1), (1, 3), (3, 1), (3, 3)]
     order += [(2, 0), (0, 2), (1, 0), (0, 1), (3, 0), (0, 3), (0, 0)]
@@ -679,35 +685,37 @@
     next(b_back)
     for n in range(5, SUM_PASSED):
         a_second(order[n])
-    for pair in order[:8]:
+    for n, pair in enumerate(order):
         a_third(pair)
-    for _ in range(3):
-        next(b_back)
-    for pair in order[8:]:
-        a_third(pair)
+        if n in (3, 7, 11):
+            next(b_back)
     next(b_back)
 
     def b_tp_sum(step):
         return remote(
             plane_sum_b.at[:, me.lanes(step)], tp_r.at[step - 1],
-            tp_send.at[step - 1], tp_recv.at[step - 1], me.tp_peer(step),
+            sum_send, tp_recv.at[0], me.tp_peer(step),
         )
 
     for step in (2, 1, 3):
         start(b_tp_sum(step))
     moe = a_sum[0].astype(F32)
+    all_here(a_ring, ar_recv.at[0])
     for pair in order[:-1]:
-        a_give(pair).wait_recv()
         moe = moe + a_ring[pair[0] * 4 + pair[1] - 1].astype(F32)
     out[:SUM_A, :] = (hid[:SUM_A, :] + moe).astype(BF16)
     moe = plane_sum[:, own_lanes]
+    all_here(tp_r, tp_recv.at[0])
     for step in (1, 3, 2):
-        b_tp_sum(step).wait_recv()
         moe = moe + tp_r[step - 1].astype(F32)
     out[SUM_A:, :] = (hid[SUM_A:, :] + moe).astype(BF16)
 
-    for copy in sent:
-        copy.wait_send()
+    for group in sends:
+        sized = {id(rs_send): part_r, id(ga_send): a_ring, id(ar_send): a_ring}.get(id(group))
+        if sized is None:
+            sized = hid_t.at[pl.ds(0, group.total // (2 * ROWS))]
+        assert group.total == 2 * math.prod(sized.shape), group.total
+        remote(sized, sized, group, rs_recv.at[0], me.sibling()).copy.wait_send()
 
 
 def local(
@@ -754,17 +762,12 @@
         pltpu.VMEM((16, SUM_A, TP_ROWS), BF16),
         pltpu.VMEM((16, SUM_A, TP_ROWS), BF16),
         pltpu.VMEM((16, 3, SUM_A, TP_ROWS), BF16),
-        dma((14,)),
-        dma((4, 6)), dma((4, 6)),
-        dma((2, 16)), dma((2, 16)), dma((2, 16)), dma((2, 16)),
-        dma((3,)), dma((3,)),
-        dma((3,)), dma((3,)),
-        dma((16,)), dma((16,)), dma((16, 3)), dma((16, 3)), dma((16,)), dma((16,)),
-        dma((2, 16)), dma((2, 16)), dma((2, 16)), dma((2, 16)),
-        dma((16,)), dma((16,)), dma((16,)), dma((16,)), dma((16, 3)), dma((16, 3)),
-        dma((15,)), dma((15,)),
-        dma((2, 2)), dma((2, 2)), dma((2, 12)), dma((2, 12)), dma((2, 3)), dma((2, 3)),
-        dma((3,)), dma((3,)),
+        dma((14,)), dma((6,)),
+        dma((2,)), dma((2, 16)), dma((2,)),
+        dma((1,)), dma((1,)),
+        dma((16,)), dma((16, 2)), dma((2, 16)), dma((1,)),
+        dma((16,)), dma((16,)), dma((16,)), dma((1,)),
+        dma((2, 2)), dma((2, 4)), dma((2,)), dma((1,)),
     ]
     return pl.pallas_call(
         kernel,

time: 105 us -> 98.7 us (0.940)
  Pallas kernels: 103 us -> 97.1 us
    pallas_call x1, Pallas kernels: 103 us -> 97.1 us  [local(): pl.pallas_call(kernel, out_shape=jax.ShapeDtypeStruct((COLS, TP_ROWS), BF...]
where the time goes in v5:
time: 98.7 us; the launch traced here: 98.6 us
  Pallas kernels  97.1 us (98%)
  local copies, waits for them, and re-layouts  1.45 us (1%)
    pallas_call x1, Pallas kernels, local(): pl.pallas_call(kernel, out_shape=jax.ShapeDtypeStruct((COLS, TP_ROWS), BF...  97.1 us

profile of v5, /device:TPU:0, one launch (start us, length us, event | category | flops | bytes accessed | tf_op | source)
XLA Modules:
  0.0 98.6 jit_solution(12202328608923781341)
XLA Ops:
  0.0 97.1 %decode_step.1 = bf16[224,128]{1,0:T(8,128)(2,1)} custom-call(s32[4]{0:T(128)} %lengths.1, bf16[4,576,128]{2,1,0:T(8,128)(2,1)} %bitcast.16, bf16[4,576,1024]{2,1,0:T(8,128)(2,1)} %bitcast.11, bf16[32,512,128]{2,1,0:T(8,128)(2,1)} %uv_hbm.1, bf16[224,4096]{1,0:T(8,128)(2,1)} %bitcast.15, bf16[224,512]{1,0:T(8,128)(2,1)} %bitcast.17, f32[56,128]{1,0:T(8,128)} %bitcast.19, ...), custom_call_target="tpu_custom_call" | custom-call | tf_op jit(solution)/shard_map/decode_step/pallas_call | solution.py:772
  97.1 1.4 %copy.14 = bf16[128,224]{0,1:T(8,128)(2,1)} copy(bf16[128,224]{0,1:T(8,128)(2,1)} %bitcast.18) | data formatting | bytes 114688

commit v6 on v5

--- a/solution.py
+++ b/solution.py
@@ -35,8 +35,7 @@
 
 SUM_A = 96
 SUM_B = 128
-PASSED = 12
-SUM_PASSED = 12
+BY_RIGHT = (2, 0)
 
 
 def tn_dot(a, b):
@@ -203,14 +202,13 @@
 
     def far(half, j):
         return remote(
-            own(half, j, 2), pass_r.at[half, j - 1], sends, pass_recv.at[half, j - 1],
-            me.second_peer(half, 1 if j == 2 else 3),
+            own(half, j, 2), pass_r.at[half, j], sends, pass_recv.at[half, j],
+            me.second_peer(half, 1 if j in BY_RIGHT else 3),
         )
 
     def near(half, j, k):
-        slot = j * 3 + k - 1
-        return remote(
-            own(half, j, k), ring_r.at[half, slot], sends, ring_recv.at[half, j],
+        return remote(
+            own(half, j, k), ring_r.at[half, j * 2 + k // 2], sends, ring_recv.at[half, j],
             me.second_peer(half, k),
         )
 
@@ -220,46 +218,33 @@
             me.first_peer(half, j),
         )
 
-    def give(j, k):
-        for half in range(2):
-            own(half, j, k)[...] = touch(half, j, k).astype(BF16)
-            start(near(half, j, k))
-
-    def give_passed(j, k):
-        for half in range(2):
-            value = touch(half, j, k)
-            far(half, j).wait_recv()
-            value = value + pass_r[half, j - 1].astype(F32)
-            own(half, j, k)[...] = value.astype(BF16)
-            start(near(half, j, k))
-
     def gathered(half, j):
         value = touch(half, j, 0)
-        steps = (1, 3) if j in (1, 2) else (1, 3, 2)
-        all_here(ring_r.at[half, pl.ds(0, len(steps))], ring_recv.at[half, j])
-        for k in steps:
-            value = value + ring_r[half, j * 3 + k - 1].astype(F32)
+        all_here(ring_r.at[half, pl.ds(0, 2)], ring_recv.at[half, j])
+        for slot in (j * 2, j * 2 + 1):
+            value = value + ring_r[half, slot].astype(F32)
         return value
 
-    for j in (2, 1):
+    for j in (2, 1, 3, 0):
         for half in range(2):
             own(half, j, 2)[...] = touch(half, j, 2).astype(BF16)
             start(far(half, j))
         yield
-    give(2, 3)
-    give(1, 1)
-    yield
-    give(3, 2)
-    give(3, 1)
-    give(3, 3)
-    yield
-    give_passed(2, 1)
-    give_passed(1, 3)
-    yield
-    give(0, 2)
-    give(0, 1)
-    give(0, 3)
-    yield
+    for j in (2, 1, 0, 3):
+        k = 3 if j in BY_RIGHT else 1
+        for half in range(2):
+            own(half, j, k)[...] = touch(half, j, k).astype(BF16)
+            start(near(half, j, k))
+        yield
+    for j in (2, 1, 3, 0):
+        k = 1 if j in BY_RIGHT else 3
+        for half in range(2):
+            value = touch(half, j, k)
+            far(half, j).wait_recv()
+            value = value + pass_r[half, j].astype(F32)
+            own(half, j, k)[...] = value.astype(BF16)
+            start(near(half, j, k))
+        yield
     for j in (2, 1, 3):
         for half in range(2):
             own(half, j, 0)[...] = gathered(half, j).astype(BF16)
@@ -460,12 +445,11 @@
         return (k, j) if half == 0 else (j, k)
 
     nearest = sorted(pairs, key=lambda pair: sum((0, 1, 2, 1)[step] for step in pair))
-    passed_on = nearest[:PASSED]
 
     def a_tp(pair, slot, lanes, step):
         ref = hid_t.at[rows_of(me.at(*pair, me.c), 0, PART_A), lanes]
         n = pair[0] * 4 + pair[1]
-        alone = pair in passed_on and slot == sum(pair) % 2
+        alone = slot == sum(pair) % 2
         return remote(
             ref, ref, gather_send, gy_recv.at[n, 0 if alone else 1], me.tp_peer(step)
         )
@@ -485,13 +469,11 @@
         a_landed.append(pair)
         start(a_tp(pair, 0, me.lanes(0), 1))
         start(a_tp(pair, 1, me.lanes(0), 3))
-        if len(a_landed) > PASSED:
-            start(a_tp(pair, 2, me.lanes(0), 2))
 
     a_passed, a_done = [0], [0]
 
     def a_pass_on(count):
-        for pair in a_landed[a_passed[0] : min(a_passed[0] + count, PASSED)]:
+        for pair in a_landed[a_passed[0] : a_passed[0] + count]:
             if sum(pair) % 2 == 0:
                 a_tp(pair, 0, me.lanes(3), 1).wait_recv()
                 start(a_tp(pair, 2, me.lanes(3), 1))
@@ -503,8 +485,7 @@
     def a_finish(count):
         for n in range(a_done[0], min(a_done[0] + count, 16)):
             pair = a_landed[n]
-            copies = 2 if pair in passed_on else 3
-            all_here(ya_pass.at[pl.ds(0, copies)], gy_recv.at[pair[0] * 4 + pair[1], 1])
+            all_here(ya_pass.at[pl.ds(0, 2)], gy_recv.at[pair[0] * 4 + pair[1], 1])
             start(a_sibling(pair, me.c))
         a_done[0] += count
 
@@ -539,16 +520,11 @@
     a_pass_on(3)
     next(b_plane)
     next(b_plane)
-    a_pass_on(4)
-    next(b_plane)
-    a_pass_on(2)
-    next(b_plane)
-    a_pass_on(2)
-    for _ in range(2):
-        a_finish(3)
+    for count in (4, 3, 3, 2):
+        a_pass_on(count)
         next(b_plane)
     for _ in range(4):
-        a_finish(2)
+        a_finish(3)
         next(b_plane)
     a_finish(16)
     all_here(hid_t.at[pl.ds(0, D // 2)], gather_sib_recv.at[0])
@@ -601,28 +577,22 @@
     def ya_near(pair, step):
         n = pair[0] * 4 + pair[1]
         return remote(
-            contrib.at[ya_rows(pair), me.lanes(step)], ya_ring.at[n, step - 1],
+            contrib.at[ya_rows(pair), me.lanes(step)], ya_ring.at[n, step // 2],
             sum_send, yr_recv.at[n], me.tp_peer(step),
         )
 
-    passed_pairs = []
+    def far_step(pair):
+        return 1 if sum(pair) % 2 == 0 else 3
 
     def a_first(pair):
         sibling_here(pair)
         at = ya_rows(pair)
         theirs = from_sib[pair[0] * 4 + pair[1], :SUM_A, :]
         contrib[at, :] = (contrib[at, :].astype(F32) + theirs.astype(F32)).astype(BF16)
-        if len(passed_pairs) < SUM_PASSED:
-            passed_pairs.append(pair)
-            far_step = 1 if sum(pair) % 2 == 0 else 3
-            start(ya_far(pair, far_step))
-            start(ya_near(pair, 4 - far_step))
-        else:
-            for step in (1, 3, 2):
-                start(ya_near(pair, step))
+        start(ya_far(pair, far_step(pair)))
 
     def a_second(pair):
-        step = 1 if sum(pair) % 2 == 0 else 3
+        step = far_step(pair)
         ya_far(pair, step).wait_recv()
         at = ya_rows(pair)
         passed = ya_pass[pair[0] * 4 + pair[1]].astype(F32)
@@ -638,10 +608,9 @@
     def a_third(pair):
         n = pair[0] * 4 + pair[1]
         value = contrib[ya_rows(pair), own_lanes].astype(F32)
-        steps = (1, 3) if pair in passed_pairs else (1, 3, 2)
-        all_here(ya_ring.at[n, pl.ds(0, len(steps))], yr_recv.at[n])
-        for step in steps:
-            value = value + ya_ring[n, step - 1].astype(F32)
+        all_here(ya_ring.at[n], yr_recv.at[n])
+        for slot in range(2):
+            value = value + ya_ring[n, slot].astype(F32)
         a_sum[n] = value.astype(BF16)
         if n:
             start(a_give(pair))
@@ -668,23 +637,24 @@
         me, b_own, b_touch, b_final, start, all_here, (b_pass, b_ring, b_line),
         (sum_send, bp_recv, br_recv, bl_recv),
     )
-    order = [(2, 2), (2, 1), (1, 2), (3, 2), (2, 3), (1, 1), (1, 3), (3, 1), (3, 3)]
-    order += [(2, 0), (0, 2), (1, 0), (0, 1), (3, 0), (0, 3), (0, 0)]
+    order = [(2, 2), (2, 1), (1, 2), (2, 3), (3, 2), (2, 0), (0, 2), (1, 1)]
+    order += [(3, 0), (0, 3), (1, 3), (3, 1), (1, 0), (0, 1), (3, 3), (0, 0)]
     for n, pair in enumerate(order):
         compute(pair)
-        if n in (3, 6, 9, 12):
+        if n in (2, 5, 7, 9):
             next(b_back)
         if n >= 3:
             a_first(order[n - 3])
-        if n >= 14:
-            a_second(order[n - 14])
     for n in range(13, 16):
         a_first(order[n])
-        a_second(order[n - 11])
-    next(b_back)
-    next(b_back)
-    for n in range(5, SUM_PASSED):
-        a_second(order[n])
+    for n, pair in enumerate(order):
+        start(ya_near(pair, 4 - far_step(pair)))
+        if n in (3, 7, 11, 15):
+            next(b_back)
+    for n, pair in enumerate(order):
+        a_second(pair)
+        if n in (1, 3, 7, 11):
+            next(b_back)
     for n, pair in enumerate(order):
         a_third(pair)
         if n in (3, 7, 11):
@@ -755,19 +725,19 @@
         pltpu.VMEM((SUM_B, ROWS), BF16),
         pltpu.VMEM((3, SUM_B, TP_ROWS), BF16),
         pltpu.VMEM((1, ROWS), F32),
-        pltpu.VMEM((2, 2, SUM_B // 2, ROWS), BF16),
-        pltpu.VMEM((2, 12, SUM_B // 2, ROWS), BF16),
+        pltpu.VMEM((2, 4, SUM_B // 2, ROWS), BF16),
+        pltpu.VMEM((2, 8, SUM_B // 2, ROWS), BF16),
         pltpu.VMEM((2, 3, SUM_B // 2, ROWS), BF16),
         pltpu.VMEM((15, SUM_A, TP_ROWS), BF16),
         pltpu.VMEM((16, SUM_A, TP_ROWS), BF16),
         pltpu.VMEM((16, SUM_A, TP_ROWS), BF16),
-        pltpu.VMEM((16, 3, SUM_A, TP_ROWS), BF16),
+        pltpu.VMEM((16, 2, SUM_A, TP_ROWS), BF16),
         dma((14,)), dma((6,)),
         dma((2,)), dma((2, 16)), dma((2,)),
         dma((1,)), dma((1,)),
         dma((16,)), dma((16, 2)), dma((2, 16)), dma((1,)),
         dma((16,)), dma((16,)), dma((16,)), dma((1,)),
-        dma((2, 2)), dma((2, 4)), dma((2,)), dma((1,)),
+        dma((2, 4)), dma((2, 4)), dma((2,)), dma((1,)),
     ]
     return pl.pallas_call(
         kernel,

time: 98.7 us -> 101 us (1.023)
  Pallas kernels: 97.1 us -> 99.2 us
    pallas_call x1, Pallas kernels: 97.1 us -> 99.2 us  [local(): pl.pallas_call(kernel, out_shape=jax.ShapeDtypeStruct((COLS, TP_ROWS), BF...]
where the time goes in v6:
time: 101 us
  Pallas kernels  99.2 us (98%)
  local copies, waits for them, and re-layouts  1.45 us (1%)
    pallas_call x1, Pallas kernels, local(): pl.pallas_call(kernel, out_shape=jax.ShapeDtypeStruct((COLS, TP_ROWS), BF...  99.2 us

profile of v6, /device:TPU:0, one launch (start us, length us, event | category | flops | bytes accessed | tf_op | source)
XLA Modules:
  0.0 100.7 jit_solution(8769683640832091364)
XLA Ops:
  0.0 99.2 %decode_step.1 = bf16[224,128]{1,0:T(8,128)(2,1)} custom-call(s32[4]{0:T(128)} %lengths.1, bf16[4,576,128]{2,1,0:T(8,128)(2,1)} %bitcast.16, bf16[4,576,1024]{2,1,0:T(8,128)(2,1)} %bitcast.11, bf16[32,512,128]{2,1,0:T(8,128)(2,1)} %uv_hbm.1, bf16[224,4096]{1,0:T(8,128)(2,1)} %bitcast.15, bf16[224,512]{1,0:T(8,128)(2,1)} %bitcast.17, f32[56,128]{1,0:T(8,128)} %bitcast.19, ...), custom_call_target="tpu_custom_call" | custom-call | tf_op jit(solution)/shard_map/decode_step/pallas_call | solution.py:742
  99.2 1.4 %copy.14 = bf16[128,224]{0,1:T(8,128)(2,1)} copy(bf16[128,224]{0,1:T(8,128)(2,1)} %bitcast.18) | data formatting | bytes 114688

commit v7 on v5

--- a/solution.py
+++ b/solution.py
@@ -28,6 +28,7 @@
 PART_B = 128
 INNER = 4096
 UNITS = 256
+CHIP = 448
 DP = 32
 
 score_scale = 192.0 ** (-0.5)
@@ -279,7 +280,7 @@
     routes_hbm, route_weights_hbm, out,
     gain, routes, route_weights, qv, cv, uv, out_w, res, down_w, gate_up_t, down_t,
     ctx, by_head, by_head_f, heads_all, part, part_b, part_r, hid, hid_t, gate_up,
-    act, contrib, from_sib, plane_sum, plane_sum_b, tp_r, weight_row,
+    gain_rows, squares, act, contrib, from_sib, plane_sum, plane_sum_b, tp_r, weight_row,
     b_pass, b_ring, b_line, a_ring, a_sum, ya_pass, ya_ring,
     load_sem, send_sems, a2a_recv, ag_recv, ag_sib_recv, rs_recv, hy_recv,
     ga_recv, gy_recv, gb_recv, gather_sib_recv,
@@ -395,10 +396,29 @@
             ref, ref, early_send, ag_sib_recv.at[half], me.sibling()
         )
 
+    def spread_gain():
+        turned_gain = pltpu.roll(gain[...], 64, axis=1)
+        low = lax.broadcasted_iota(jnp.int32, (1, 128), 1) < 64
+        for chip in range(D // CHIP):
+            for q in range(4):
+                at, odd = divmod(chip * CHIP + q * 128, 128)
+                row = gain[at : at + 1, :]
+                if odd:
+                    row = turned_gain[at : at + 1, :]
+                    if q < 3:
+                        row = jnp.where(low, row, turned_gain[at + 1 : at + 2, :])
+                gain_rows[q, chip : chip + 1, :] = row
+
+    def turn_chip(chip, carry):
+        for q in range(4):
+            width = 128 if q < 3 else 64
+            rows = contrib[pl.ds(pl.multiple_of(chip * CHIP + q * 128, 64), width), :]
+            turned = rows.astype(F32).T * gain_rows[q, pl.ds(chip, 1), :][:, :width]
+            gate_up_t[chip, :, q * 128 : q * 128 + width] = turned.astype(BF16)
+        return carry
+
     def turn_step(i, carry):
         at = pl.ds(pl.multiple_of(i * 128, 128), 128)
-        turned = contrib[at, :].astype(F32).T * gain[pl.ds(i, 1), :]
-        gate_up_t[:, at] = turned.astype(BF16)
         down_t[at, :] = down_w[:, at].astype(F32).T.astype(BF16)
         return carry
 
@@ -412,9 +432,11 @@
         if turned_to == 0:
             for name in ("gate", "up", "down", "gain"):
                 ready(name)
-        upto = min(turned_to + 7, D // 128)
-        lax.fori_loop(turned_to, upto, turn_step, 0)
-        turned_to = upto
+            spread_gain()
+        if turned_to < D // 128:
+            lax.fori_loop(turned_to // 7 * 2, turned_to // 7 * 2 + 2, turn_chip, 0)
+            lax.fori_loop(turned_to, turned_to + 7, turn_step, 0)
+            turned_to += 7
 
     ready("out_w")
     part[...] = jnp.zeros_like(part)
@@ -459,7 +481,7 @@
     def pair_of(half, j, k):
         return (k, j) if half == 0 else (j, k)
 
-    nearest = sorted(pairs, key=lambda pair: sum((0, 1, 2, 1)[step] for step in pair))
+    nearest = sorted(pairs, key=lambda pair: (2 in pair, sum((0, 1, 2, 1)[step] for step in pair)))
     passed_on = nearest[:PASSED]
 
     def a_tp(pair, slot, lanes, step):
@@ -472,7 +494,8 @@
 
     def a_sibling(pair, c):
         ref = hid_t.at[rows_of(me.at(*pair, c), 0, PART_A), :]
-        return remote(ref, ref, gather_send, gather_sib_recv.at[0], me.sibling())
+        late = 1 if 2 in pair else 0
+        return remote(ref, ref, gather_send, gather_sib_recv.at[late], me.sibling())
 
     def a_plane(pair):
         ref = hid_t.at[rows_of(d, 0, PART_A), own_lanes]
@@ -510,7 +533,8 @@
 
     def b_sibling(half, j, k, c):
         ref = b_block(half, me.block(half, j, k, c))
-        return remote(ref, ref, gather_send, gather_sib_recv.at[0], me.sibling())
+        late = 1 if 2 in (j, k) else 0
+        return remote(ref, ref, gather_send, gather_sib_recv.at[late], me.sibling())
 
     def b_tp(lanes, step):
         ref = hid_t.at[rows_of(d, PART_A, PART_B), lanes]
@@ -544,26 +568,38 @@
     a_pass_on(2)
     next(b_plane)
     a_pass_on(2)
-    for _ in range(2):
-        a_finish(3)
-        next(b_plane)
-    for _ in range(4):
+    next(b_plane)
+    next(b_plane)
+
+    gate_up[...] = jnp.zeros_like(gate_up)
+    squares[...] = jnp.zeros_like(squares)
+
+    def expert(pair):
+        chip = me.at(*pair, 0) // 2
+        rows = hid_t[pl.ds(pl.multiple_of(chip * CHIP, 64), CHIP), :]
+        gate_up[...] += jnp.dot(gate_up_t[chip], rows, preferred_element_type=F32)
+        wide = rows.astype(F32)
+        squares[...] += jnp.sum((wide * wide).reshape(CHIP // 8, 8, ROWS), axis=0)
+
+    early = nearest[:9]
+    a_finish(9)
+    next(b_plane)
+    a_finish(1)
+    next(b_plane)
+    all_here(hid_t.at[pl.ds(0, 9 * COLS)], gather_sib_recv.at[0])
+    for n in range(2):
+        for pair in early[3 * n : 3 * n + 3]:
+            expert(pair)
         a_finish(2)
         next(b_plane)
     a_finish(16)
-    all_here(hid_t.at[pl.ds(0, D // 2)], gather_sib_recv.at[0])
-
-    gate_up[...] = jnp.zeros_like(gate_up)
-
-    def expert_step(k, squares):
-        at = pl.ds(pl.multiple_of(k * 1024, 1024), 1024)
-        rows = hid_t[at, :]
-        gate_up[...] += jnp.dot(gate_up_t[:, at], rows, preferred_element_type=F32)
-        wide = rows.astype(F32)
-        return squares + jnp.sum((wide * wide).reshape(128, 8, ROWS), axis=0)
-
-    squares = lax.fori_loop(0, D // 1024, expert_step, jnp.zeros((8, ROWS), F32))
-    inverse_rms = lax.rsqrt(jnp.sum(squares, axis=0, keepdims=True) * (1.0 / D) + epsilon)
+    for pair in early[6:]:
+        expert(pair)
+    all_here(hid_t.at[pl.ds(0, 7 * COLS)], gather_sib_recv.at[1])
+    for pair in nearest[9:]:
+        expert(pair)
+
+    inverse_rms = lax.rsqrt(jnp.sum(squares[...], axis=0, keepdims=True) * (1.0 / D) + epsilon)
     gate_proj = gate_up[:UNITS, :] * inverse_rms
     up_proj = gate_up[UNITS:, :] * inverse_rms
     silu = gate_proj / (1.0 + jnp.exp(-gate_proj))
@@ -736,7 +772,7 @@
         pltpu.VMEM((COLS, INNER), BF16),
         pltpu.VMEM((COLS, TP_ROWS), BF16),
         pltpu.VMEM((UNITS, D), BF16),
-        pltpu.VMEM((2 * UNITS, D), BF16),
+        pltpu.VMEM((D // CHIP, 2 * UNITS, CHIP), BF16),
         pltpu.VMEM((D, UNITS), BF16),
         pltpu.VMEM((OWN_ROWS, HEADS, LAT), BF16),
         pltpu.VMEM((DP_ROWS, OWN_HEADS, LAT), BF16),
@@ -748,6 +784,8 @@
         pltpu.VMEM((COLS, TP_ROWS), F32),
         pltpu.VMEM((D, ROWS), BF16),
         pltpu.VMEM((2 * UNITS, ROWS), F32),
+        pltpu.VMEM((4, D // CHIP, 128), F32),
+        pltpu.VMEM((8, ROWS), F32),
         pltpu.VMEM((UNITS, ROWS), BF16),
         pltpu.VMEM((D, ROWS), BF16),
         pltpu.VMEM((16, COLS, ROWS), BF16),
@@ -765,7 +803,7 @@
         dma((14,)), dma((6,)),
         dma((2,)), dma((2, 16)), dma((2,)),
         dma((1,)), dma((1,)),
-        dma((16,)), dma((16, 2)), dma((2, 16)), dma((1,)),
+        dma((16,)), dma((16, 2)), dma((2, 16)), dma((2,)),
         dma((16,)), dma((16,)), dma((16,)), dma((1,)),
         dma((2, 2)), dma((2, 4)), dma((2,)), dma((1,)),
     ]

time: 98.7 us -> 98.4 us (level)
  no operation moved by 1% of the time
where the time goes in v7:
time: 98.4 us; the launch traced here: 98.3 us
  Pallas kernels  96.8 us (98%)
  local copies, waits for them, and re-layouts  1.45 us (1%)
    pallas_call x1, Pallas kernels, local(): pl.pallas_call(kernel, out_shape=jax.ShapeDtypeStruct((COLS, TP_ROWS), BF...  96.8 us

profile of v7, /device:TPU:0, one launch (start us, length us, event | category | flops | bytes accessed | tf_op | source)
XLA Modules:
  0.0 98.3 jit_solution(1593854114958960153)
XLA Ops:
  0.0 96.8 %decode_step.1 = bf16[224,128]{1,0:T(8,128)(2,1)} custom-call(s32[4]{0:T(128)} %lengths.1, bf16[4,576,128]{2,1,0:T(8,128)(2,1)} %bitcast.16, bf16[4,576,1024]{2,1,0:T(8,128)(2,1)} %bitcast.11, bf16[32,512,128]{2,1,0:T(8,128)(2,1)} %uv_hbm.1, bf16[224,4096]{1,0:T(8,128)(2,1)} %bitcast.15, bf16[224,512]{1,0:T(8,128)(2,1)} %bitcast.17, f32[56,128]{1,0:T(8,128)} %bitcast.19, ...), custom_call_target="tpu_custom_call" | custom-call | tf_op jit(solution)/shard_map/decode_step/pallas_call | solution.py:810
  96.8 1.4 %copy.14 = bf16[128,224]{0,1:T(8,128)(2,1)} copy(bf16[128,224]{0,1:T(8,128)(2,1)} %bitcast.18) | data formatting | bytes 114688

commit v8 on v7

--- a/solution.py
+++ b/solution.py
@@ -330,15 +330,15 @@
     ready("q")
     for i in range(OWN_ROWS):
         ready(("cache", i))
-        if i == 1:
+        if i == 0:
+            load("gain", gain_hbm, gain, 11)
+            load("gate", gate_hbm, contrib.at[:, pl.ds(0, UNITS)], 8)
+            load("up", up_hbm, contrib.at[:, pl.ds(UNITS, UNITS)], 9)
+            load("down", down_hbm, down_w, 10)
+        if i == 2:
             load("uv", uv_hbm, uv, 5)
             load("out_w", out_w_hbm, out_w, 6)
             load("res", residual_hbm.at[:, own_lanes], res, 7)
-        if i == 2:
-            load("gate", gate_hbm, contrib.at[:, pl.ds(0, UNITS)], 8)
-            load("up", up_hbm, contrib.at[:, pl.ds(UNITS, UNITS)], 9)
-            load("down", down_hbm, down_w, 10)
-            load("gain", gain_hbm, gain, 11)
             load("routes", routes_hbm, routes, 12)
             load("route_weights", route_weights_hbm, route_weights, 13)
         scores = tn_dot(qv[i], cv[i]) * score_scale
@@ -361,6 +361,37 @@
         for step in (2, 1, 3):
             start(heads_out(i, 1, step))
 
+    def spread_gain():
+        turned_gain = pltpu.roll(gain[...], 64, axis=1)
+        low = lax.broadcasted_iota(jnp.int32, (1, 128), 1) < 64
+        for chip in range(D // CHIP):
+            for q in range(4):
+                at, odd = divmod(chip * CHIP + q * 128, 128)
+                row = gain[at : at + 1, :]
+                if odd:
+                    row = turned_gain[at : at + 1, :]
+                    if q < 3:
+                        row = jnp.where(low, row, turned_gain[at + 1 : at + 2, :])
+                gain_rows[q, chip : chip + 1, :] = row
+
+    def turn_chip(chip, carry):
+        for q in range(4):
+            width = 128 if q < 3 else 64
+            rows = contrib[pl.ds(pl.multiple_of(chip * CHIP + q * 128, 64), width), :]
+            turned = rows.astype(F32).T * gain_rows[q, pl.ds(chip, 1), :][:, :width]
+            gate_up_t[chip, :, q * 128 : q * 128 + width] = turned.astype(BF16)
+        return carry
+
+    def turn_step(i, carry):
+        at = pl.ds(pl.multiple_of(i * 128, 128), 128)
+        down_t[at, :] = down_w[:, at].astype(F32).T.astype(BF16)
+        return carry
+
+    for name in ("gain", "gate", "up", "down"):
+        ready(name)
+    spread_gain()
+    lax.fori_loop(0, D // CHIP, turn_chip, 0)
+
     ready("uv")
     own_rows = pl.ds(pl.multiple_of(d * DP_ROWS, DP_ROWS), DP_ROWS)
 
@@ -396,45 +427,14 @@
             ref, ref, early_send, ag_sib_recv.at[half], me.sibling()
         )
 
-    def spread_gain():
-        turned_gain = pltpu.roll(gain[...], 64, axis=1)
-        low = lax.broadcasted_iota(jnp.int32, (1, 128), 1) < 64
-        for chip in range(D // CHIP):
-            for q in range(4):
-                at, odd = divmod(chip * CHIP + q * 128, 128)
-                row = gain[at : at + 1, :]
-                if odd:
-                    row = turned_gain[at : at + 1, :]
-                    if q < 3:
-                        row = jnp.where(low, row, turned_gain[at + 1 : at + 2, :])
-                gain_rows[q, chip : chip + 1, :] = row
-
-    def turn_chip(chip, carry):
-        for q in range(4):
-            width = 128 if q < 3 else 64
-            rows = contrib[pl.ds(pl.multiple_of(chip * CHIP + q * 128, 64), width), :]
-            turned = rows.astype(F32).T * gain_rows[q, pl.ds(chip, 1), :][:, :width]
-            gate_up_t[chip, :, q * 128 : q * 128 + width] = turned.astype(BF16)
-        return carry
-
-    def turn_step(i, carry):
-        at = pl.ds(pl.multiple_of(i * 128, 128), 128)
-        down_t[at, :] = down_w[:, at].astype(F32).T.astype(BF16)
-        return carry
-
-    turned_to = 0
     heads_plane = gather_plane(
         me, head_block, start, (early_send, ag_recv), lambda *at: start(head_sibling(*at, me.c))
     )
     next(heads_plane)
     project(1)
+    turned_to = 0
     for step in heads_plane:
-        if turned_to == 0:
-            for name in ("gate", "up", "down", "gain"):
-                ready(name)
-            spread_gain()
         if turned_to < D // 128:
-            lax.fori_loop(turned_to // 7 * 2, turned_to // 7 * 2 + 2, turn_chip, 0)
             lax.fori_loop(turned_to, turned_to + 7, turn_step, 0)
             turned_to += 7
 
@@ -442,13 +442,13 @@
     part[...] = jnp.zeros_like(part)
 
     def out_step(k, carry):
-        at = pl.ds(pl.multiple_of(k * 512, 512), 512)
+        at = pl.ds(pl.multiple_of(k * 1024, 1024), 1024)
         part[...] += nt_dot(out_w[:, at], heads_all[:, at])
         return carry
 
     for half in range(2):
         all_here(heads_all.at[pl.ds(0, ROWS // 2), pl.ds(0, INNER // 2)], ag_sib_recv.at[half])
-        lax.fori_loop(half * 4, half * 4 + 4, out_step, 0)
+        lax.fori_loop(half * 2, half * 2 + 2, out_step, 0)
     for block in range(4):
         part_b[block] = part[:, block * TP_ROWS : (block + 1) * TP_ROWS].astype(BF16)
     for step in (2, 1, 3):

time: 98.4 us -> 96.4 us (0.980)
  Pallas kernels: 96.8 us -> 94.7 us
    pallas_call x1, Pallas kernels: 96.8 us -> 94.7 us  [local(): pl.pallas_call(kernel, out_shape=jax.ShapeDtypeStruct((COLS, TP_ROWS), BF...]
where the time goes in v8:
time: 96.4 us; the launch traced here: 96.2 us
  Pallas kernels  94.7 us (98%)
  local copies, waits for them, and re-layouts  1.45 us (2%)
    pallas_call x1, Pallas kernels, local(): pl.pallas_call(kernel, out_shape=jax.ShapeDtypeStruct((COLS, TP_ROWS), BF...  94.7 us

profile of v8, /device:TPU:0, one launch (start us, length us, event | category | flops | bytes accessed | tf_op | source)
XLA Modules:
  0.0 96.2 jit_solution(444238582301256234)
XLA Ops:
  0.0 94.7 %decode_step.1 = bf16[224,128]{1,0:T(8,128)(2,1)} custom-call(s32[4]{0:T(128)} %lengths.1, bf16[4,576,128]{2,1,0:T(8,128)(2,1)} %bitcast.16, bf16[4,576,1024]{2,1,0:T(8,128)(2,1)} %bitcast.11, bf16[32,512,128]{2,1,0:T(8,128)(2,1)} %uv_hbm.1, bf16[224,4096]{1,0:T(8,128)(2,1)} %bitcast.15, bf16[224,512]{1,0:T(8,128)(2,1)} %bitcast.17, f32[56,128]{1,0:T(8,128)} %bitcast.19, ...), custom_call_target="tpu_custom_call" | custom-call | tf_op jit(solution)/shard_map/decode_step/pallas_call | solution.py:810
  94.7 1.4 %copy.14 = bf16[128,224]{0,1:T(8,128)(2,1)} copy(bf16[128,224]{0,1:T(8,128)(2,1)} %bitcast.18) | data formatting | bytes 114688

commit v9 on v8

--- a/solution.py
+++ b/solution.py
@@ -34,8 +34,8 @@
 score_scale = 192.0 ** (-0.5)
 epsilon = 1e-06
 
-SUM_A = 96
-SUM_B = 128
+SUM_A = 64
+SUM_B = 160
 PASSED = 12
 SUM_PASSED = 12
 
@@ -291,8 +291,8 @@
     own_lanes = pl.ds(pl.multiple_of(y * TP_ROWS, TP_ROWS), TP_ROWS)
 
     loads = {}
-    sends = [Sends(send_sems, group) for group in range(6)]
-    early_send, rs_send, gather_send, ga_send, sum_send, ar_send = sends
+    sends = [Sends(send_sems, group) for group in range(7)]
+    early_send, rs_send, gather_send, ga_send, sum_send, ar_send, tp_send = sends
 
     def load(name, src, dst, index):
         copy = pltpu.make_async_copy(src, dst, load_sem.at[index])
@@ -527,7 +527,7 @@
         for n in range(a_done[0], min(a_done[0] + count, 16)):
             pair = a_landed[n]
             copies = 2 if pair in passed_on else 3
-            all_here(ya_pass.at[pl.ds(0, copies)], gy_recv.at[pair[0] * 4 + pair[1], 1])
+            all_here(hid_t.at[pl.ds(0, PART_A * copies), pl.ds(0, TP_ROWS)], gy_recv.at[pair[0] * 4 + pair[1], 1])
             start(a_sibling(pair, me.c))
         a_done[0] += count
 
@@ -552,7 +552,7 @@
         opposite = ((4 - pair[0]) % 4, (4 - pair[1]) % 4)
         a_plane(opposite).wait_recv()
         a_here(pair)
-    all_here(tp_r, hy_recv.at[0])
+    all_here(hid_t.at[pl.ds(0, 3 * PART_B), pl.ds(0, TP_ROWS)], hy_recv.at[0])
     next(b_plane)
     next(b_plane)
     a_pass_on(1)
@@ -730,7 +730,7 @@
     def b_tp_sum(step):
         return remote(
             plane_sum_b.at[:, me.lanes(step)], tp_r.at[step - 1],
-            sum_send, tp_recv.at[0], me.tp_peer(step),
+            tp_send, tp_recv.at[0], me.tp_peer(step),
         )
 
     for step in (2, 1, 3):
@@ -747,7 +747,10 @@
     out[SUM_A:, :] = (hid[SUM_A:, :] + moe).astype(BF16)
 
     for group in sends:
-        sized = {id(rs_send): part_r, id(ga_send): a_ring, id(ar_send): a_ring}.get(id(group))
+        a_blocks = hid_t.at[pl.ds(0, 15 * PART_A), pl.ds(0, TP_ROWS)]
+        sized = {
+            id(rs_send): part_r, id(ga_send): a_blocks, id(ar_send): a_ring, id(tp_send): tp_r
+        }.get(id(group))
         if sized is None:
             sized = hid_t.at[pl.ds(0, group.total // (2 * ROWS))]
         assert group.total == 2 * math.prod(sized.shape), group.total
@@ -800,7 +803,7 @@
         pltpu.VMEM((16, SUM_A, TP_ROWS), BF16),
         pltpu.VMEM((16, SUM_A, TP_ROWS), BF16),
         pltpu.VMEM((16, 3, SUM_A, TP_ROWS), BF16),
-        dma((14,)), dma((6,)),
+        dma((14,)), dma((7,)),
         dma((2,)), dma((2, 16)), dma((2,)),
         dma((1,)), dma((1,)),
         dma((16,)), dma((16, 2)), dma((2, 16)), dma((2,)),

time: 96.4 us -> 96.4 us (level)
  no operation moved by 1% of the time
where the time goes in v9:
time: 96.4 us; the launch traced here: 96 us
  Pallas kernels  94.5 us (98%)
  local copies, waits for them, and re-layouts  1.45 us (2%)
    pallas_call x1, Pallas kernels, local(): pl.pallas_call(kernel, out_shape=jax.ShapeDtypeStruct((COLS, TP_ROWS), BF...  94.5 us

profile of v9, /device:TPU:0, one launch (start us, length us, event | category | flops | bytes accessed | tf_op | source)
XLA Modules:
  0.0 96.0 jit_solution(12334875538708069828)
XLA Ops:
  0.0 94.5 %decode_step.1 = bf16[224,128]{1,0:T(8,128)(2,1)} custom-call(s32[4]{0:T(128)} %lengths.1, bf16[4,576,128]{2,1,0:T(8,128)(2,1)} %bitcast.16, bf16[4,576,1024]{2,1,0:T(8,128)(2,1)} %bitcast.11, bf16[32,512,128]{2,1,0:T(8,128)(2,1)} %uv_hbm.1, bf16[224,4096]{1,0:T(8,128)(2,1)} %bitcast.15, bf16[224,512]{1,0:T(8,128)(2,1)} %bitcast.17, f32[56,128]{1,0:T(8,128)} %bitcast.19, ...), custom_call_target="tpu_custom_call" | custom-call | tf_op jit(solution)/shard_map/decode_step/pallas_call | solution.py:813
  94.5 1.4 %copy.14 = bf16[128,224]{0,1:T(8,128)(2,1)} copy(bf16[128,224]{0,1:T(8,128)(2,1)} %bitcast.18) | data formatting | bytes 114688
